TPU v7x, 32 devices: a whole 2x2x4 slice. The times are simulated.
32 devices in a mesh: row: 8 (over y, x, core), col: 4 (over z).
Axes of the slice: x: 2, y: 2, z: 4, core: 2. Of those that a mesh axis runs over, the one named last changes fastest.
Arguments:
- field: bfloat16 [64, 64, 512], P('row', 'col'), may hold values from -6 to 6
- in_weight: bfloat16 [512, 2048], P(None, 'row'), may hold values from -0.25 to 0.25
- conv_weight: float32 [3, 3, 1024], replicated, may hold values from -2 to 2
- proj_weight: bfloat16 [1024, 256], replicated, may hold values from -0.1875 to 0.1875
- dt_weight: bfloat16 [4, 32, 1024], replicated, may hold values from -1 to 1
- dt_bias: float32 [4, 1024], replicated, may hold values from -7 to -2
- decay_rate: float32 [4, 16, 1024], replicated, may hold values from 0.5 to 2
- skip_gain: float32 [4, 1024], replicated, may hold values from 0.1 to 1.9
- norm_gain: float32 [1024], replicated, may hold values from 0.1 to 1.9
- out_weight: bfloat16 [1024, 512], P('col'), may hold values from -0.1875 to 0.1875
- grad_out: bfloat16 [64, 64, 512], P('row', 'col'), may hold values from -6 to 6
Outputs:
- result: bfloat16 [64, 64, 512], P('row', 'col')
- grad_field: float32 [64, 64, 512], P('row', 'col')
- grad_in_weight: float32 [512, 2048], P(None, 'row')
- grad_out_weight: float32 [1024, 512], P('col')
All inputs are finite; a program needn't handle non-finite values.
Results may differ from a plain program's by a relative error of at most 0.0073.
Values may be sent and summed in bfloat16 or wider, within the bound.
A program may use at most 256 MiB of HBM per device.

v0:
```python
import math

import jax
import jax.numpy as jnp
from jax import lax
from jax.experimental import pallas as pl
from jax.experimental.pallas import tpu as pltpu
from jax.sharding import PartitionSpec as P

DT_FLOOR = 0.004
NORM_EPS = 1e-05
LOG2E = math.log2(math.e)
LN2 = math.log(2.0)
LANES = 128
F32 = jnp.float32
BF16 = jnp.bfloat16


def softplus(v):
    return jnp.maximum(v, 0.0) + jnp.log1p(jnp.exp(-jnp.abs(v)))


def fill_steps(proj_ref, dtw_ref, bias_ref, raw_ref, step_ref):
    length, lines, width = proj_ref.shape
    chunk = 16

    @pl.loop(0, length // chunk)
    def _(c):
        rows = proj_ref[pl.ds(c * chunk, chunk)].reshape(chunk * lines, width)
        raw = jnp.dot(rows, dtw_ref[...], preferred_element_type=F32) + bias_ref[0:1, :]
        raw = raw.reshape(chunk, lines, raw.shape[-1])
        if raw_ref is not None:
            raw_ref[pl.ds(c * chunk, chunk)] = raw
        step_ref[pl.ds(c * chunk, chunk)] = DT_FLOOR + softplus(raw)


def column(values, i, like):
    return jnp.broadcast_to(values[:, i : i + 1], like.shape)


def forward_kernel(rank, states, act_ref, proj_ref, dtw_ref, bias_ref, rate_ref, skip_ref, y_ref, start_ref, step_ref):
    k = pl.program_id(0)
    length, lines, width = act_ref.shape
    fill_steps(proj_ref, dtw_ref, bias_ref, None, step_ref)
    zero = jnp.zeros((lines, width), F32)

    def place(i):
        return jnp.where(k == 0, i, length - 1 - i)

    def first(i, carry):
        state, total = carry
        p = place(i)
        step = step_ref[p]
        drive = step * act_ref[p].astype(F32)
        coef = proj_ref[p].astype(F32)
        state = tuple(
            jnp.exp2(step * rate_ref[n]) * state[n] + drive * column(coef, rank + n, step)
            for n in range(states)
        )
        return state, total + step

    state, total = lax.fori_loop(0, length, first, ((zero,) * states, zero))
    closed = []
    for n in range(states):
        one = state[n] / (1.0 - jnp.exp2(total * rate_ref[n]))
        start_ref[n] = one
        closed.append(one)

    @pl.when(k == 0)
    def _():
        y_ref[...] = jnp.zeros_like(y_ref)

    skip = jnp.broadcast_to(skip_ref[0:1, :], (lines, width))

    def second(i, state):
        p = place(i)
        step = step_ref[p]
        act = act_ref[p].astype(F32)
        drive = step * act
        coef = proj_ref[p].astype(F32)
        y = y_ref[p] + skip * act
        new = []
        for n in range(states):
            one = jnp.exp2(step * rate_ref[n]) * state[n] + drive * column(coef, rank + n, step)
            y = y + one * column(coef, rank + states + n, step)
            new.append(one)
        y_ref[p] = y
        return tuple(new)

    lax.fori_loop(0, length, second, tuple(closed))


def backward_kernel(
    rank, states, act_ref, proj_ref, dtw_ref, dtwt_ref, bias_ref, rate_ref, skip_ref, start_ref, gy_ref, pick_ref,
    dact_ref, dproj_ref, raw_ref, step_ref, h_ref, a_ref, prod_ref, draw_ref,
):
    k = pl.program_id(0)
    length, lines, width = act_ref.shape
    fill_steps(proj_ref, dtw_ref, bias_ref, raw_ref, step_ref)
    zero = jnp.zeros((lines, width), F32)

    def place(i):
        return jnp.where(k == 0, i, length - 1 - i)

    for n in range(states):
        h_ref[0, n] = start_ref[n]

    def replay(i, carry):
        state, total = carry
        p = place(i)
        step = step_ref[p]
        drive = step * act_ref[p].astype(F32)
        coef = proj_ref[p].astype(F32)
        new = []
        for n in range(states):
            decay = jnp.exp2(step * rate_ref[n])
            one = decay * state[n] + drive * column(coef, rank + n, step)
            a_ref[i, n] = decay
            h_ref[i + 1, n] = one
            new.append(one)
        return tuple(new), total + step

    _, total = lax.fori_loop(0, length, replay, (tuple(start_ref[n] for n in range(states)), zero))

    def adjoint(j, back):
        i = length - 1 - j
        p = place(i)
        gy = gy_ref[p].astype(F32)
        coef = proj_ref[p].astype(F32)
        return tuple(
            a_ref[i, n] * (back[n] + gy * column(coef, rank + states + n, gy)) for n in range(states)
        )

    back = lax.fori_loop(0, length, adjoint, (zero,) * states)
    back = tuple(back[n] / (1.0 - jnp.exp2(total * rate_ref[n])) for n in range(states))

    @pl.when(k == 0)
    def _():
        dact_ref[...] = jnp.zeros_like(dact_ref)

    skip = jnp.broadcast_to(skip_ref[0:1, :], (lines, width))

    def last(j, back):
        i = length - 1 - j
        p = place(i)
        gy = gy_ref[p].astype(F32)
        coef = proj_ref[p].astype(F32)
        step = step_ref[p]
        act = act_ref[p].astype(F32)
        drive = step * act
        ddrive = zero
        dstep = zero
        new = []
        for n in range(states):
            lam = back[n] + gy * column(coef, rank + states + n, gy)
            prod_ref[p, :, pl.ds(n * width, width)] = (drive * lam).astype(BF16)
            prod_ref[p, :, pl.ds((states + n) * width, width)] = (gy * h_ref[i + 1, n]).astype(BF16)
            ddrive = ddrive + lam * column(coef, rank + n, gy)
            carried = a_ref[i, n] * lam
            dstep = dstep + (carried * h_ref[i, n]) * rate_ref[n]
            new.append(carried)
        dstep = LN2 * dstep + act * ddrive
        dact_ref[p] = dact_ref[p] + step * ddrive + skip * gy
        draw_ref[p] = (dstep / (1.0 + jnp.exp(-raw_ref[p]))).astype(BF16)
        return tuple(new)

    lax.fori_loop(0, length, last, back)
    chunk = 8

    @pl.loop(0, length // chunk)
    def _(c):
        at = pl.ds(c * chunk, chunk)
        prods = prod_ref[at].reshape(chunk * lines, prod_ref.shape[-1])
        raws = draw_ref[at].reshape(chunk * lines, width)
        out = jnp.dot(prods, pick_ref[...], preferred_element_type=F32)
        out = out + jnp.dot(raws, dtwt_ref[...], preferred_element_type=F32)
        dproj_ref[at] = out.reshape(chunk, lines, out.shape[-1])


def whole_spec(shape):
    return pl.BlockSpec(shape, lambda k: (0,) * len(shape))


def each_spec(shape):
    return pl.BlockSpec((None,) + shape, lambda k: (k,) + (0,) * len(shape))


def run_forward(act, proj, params):
    dtw, dtwt, bias, rates, skip, rank, states = params
    length, lines, width = act.shape
    coefs = proj.shape[-1]
    work = 2 * 2 * length * lines * width * states
    return pl.pallas_call(
        lambda *refs: forward_kernel(rank, states, *refs),
        grid=(2,),
        in_specs=[
            whole_spec(act.shape),
            each_spec((length, lines, coefs)),
            each_spec((coefs, width)),
            each_spec((8, width)),
            each_spec((states, lines, width)),
            each_spec((8, width)),
        ],
        out_specs=[whole_spec(act.shape), each_spec((states, lines, width))],
        out_shape=[
            jax.ShapeDtypeStruct(act.shape, F32),
            jax.ShapeDtypeStruct((2, states, lines, width), F32),
        ],
        scratch_shapes=[pltpu.VMEM(act.shape, F32)],
        compiler_params=pltpu.CompilerParams(vmem_limit_bytes=40 * 2**20),
        cost_estimate=pl.CostEstimate(flops=10 * work, bytes_accessed=4 * act.size * 4, transcendentals=work),
        name="scan_forward",
    )(act, proj, dtw, bias, rates, skip)


def run_backward(act, proj, params, start, gy, pick):
    dtw, dtwt, bias, rates, skip, rank, states = params
    length, lines, width = act.shape
    coefs = proj.shape[-1]
    work = 2 * 3 * length * lines * width * states
    return pl.pallas_call(
        lambda *refs: backward_kernel(rank, states, *refs),
        grid=(2,),
        in_specs=[
            whole_spec(act.shape),
            each_spec((length, lines, coefs)),
            each_spec((coefs, width)),
            each_spec((width, coefs)),
            each_spec((8, width)),
            each_spec((states, lines, width)),
            each_spec((8, width)),
            each_spec((states, lines, width)),
            whole_spec(act.shape),
            whole_spec(pick.shape),
        ],
        out_specs=[whole_spec(act.shape), each_spec((length, lines, coefs))],
        out_shape=[
            jax.ShapeDtypeStruct(act.shape, F32),
            jax.ShapeDtypeStruct((2, length, lines, coefs), F32),
        ],
        scratch_shapes=[
            pltpu.VMEM(act.shape, F32),
            pltpu.VMEM(act.shape, F32),
            pltpu.VMEM((length + 1, states, lines, width), F32),
            pltpu.VMEM((length, states, lines, width), F32),
            pltpu.VMEM((length, lines, 2 * states * width), BF16),
            pltpu.VMEM(act.shape, BF16),
        ],
        compiler_params=pltpu.CompilerParams(vmem_limit_bytes=60 * 2**20),
        cost_estimate=pl.CostEstimate(flops=10 * work, bytes_accessed=8 * act.size * 4, transcendentals=work),
        name="scan_backward",
    )(act, proj, dtw, dtwt, bias, rates, skip, start, gy, pick)


def pad_to(values, axis, size, fill=0.0):
    missing = size - values.shape[axis]
    if missing == 0:
        return values
    pads = [(0, 0)] * values.ndim
    pads[axis] = (0, missing)
    return jnp.pad(values, pads, constant_values=fill)


def swap(values):
    return jnp.swapaxes(values, 0, 1)


def weight_moves(peers):
    half = peers // 2
    one = [(r, 2 * r if r < half else 2 * (r - half) + 1) for r in range(peers)]
    two = [(r, 2 * r + 1 if r < half else 2 * (r - half)) for r in range(peers)]
    return one, two


def reverse_moves(moves):
    return [(b, a) for a, b in moves]


def col_halo(cells):
    peers = lax.axis_size("col")
    up = [(i, (i + 1) % peers) for i in range(peers)]
    down = [((i + 1) % peers, i) for i in range(peers)]
    before = lax.ppermute(cells[:, -1:], "col", up)
    after = lax.ppermute(cells[:, :1], "col", down)
    wide = jnp.concatenate([before, cells, after], axis=1)
    return jnp.concatenate([wide[-1:], wide, wide[:1]], axis=0)


def local(
    field, in_weight, conv_weight, proj_weight, dt_weight, dt_bias, decay_rate, skip_gain, norm_gain, out_weight, grad_out,
):
    rows, cols, c_dim = field.shape
    dirs, rank, e_dim = dt_weight.shape
    states = decay_rate.shape[1]
    coefs = rank + 2 * states
    nr, nc = lax.axis_size("row"), lax.axis_size("col")
    me = lax.axis_index("row")
    all_rows, width = rows * nr, e_dim // nr
    even = me % 2 == 0
    low = me < nr // 2
    moves_one, moves_two = weight_moves(nr)

    def mine(values):
        return lax.dynamic_slice_in_dim(values, me * width, width, axis=values.ndim - 1)

    field_all = lax.all_gather(field, "row", axis=0, tiled=True)
    left, right = in_weight[:, :width], in_weight[:, width:]
    got_one = lax.ppermute(jnp.where(low, left, right), "row", moves_one)
    got_two = lax.ppermute(jnp.where(low, right, left), "row", moves_two)
    w_mine = jnp.concatenate(
        [jnp.where(even, got_one, got_two), jnp.where(even, got_two, got_one)], axis=1
    )
    field_flat = field_all.reshape(-1, c_dim)
    xz = jnp.dot(field_flat, w_mine, preferred_element_type=F32).astype(BF16).reshape(all_rows, cols, 2 * width)
    source, gate = xz[..., :width], xz[..., width:].astype(F32)
    grad_all = lax.all_gather(grad_out, "row", axis=0, tiled=True)
    out_full = lax.all_gather(out_weight, "col", axis=0, tiled=True)
    w_perm = lax.all_gather(w_mine, "row", axis=1, tiled=True)

    taps = mine(conv_weight)
    padded = col_halo(source)
    convolved = jnp.zeros(source.shape, F32)
    for a in range(3):
        for b in range(3):
            convolved = convolved + padded[a : a + all_rows, b : b + cols].astype(F32) * taps[a, b]
    active = jax.nn.silu(convolved).astype(BF16)

    act_cells = lax.all_to_all(active, "row", 0, 2, tiled=True)
    proj_cells = jnp.dot(act_cells.reshape(-1, e_dim), proj_weight, preferred_element_type=F32)
    proj = lax.all_gather(
        proj_cells.astype(BF16).reshape(rows, cols, dirs * coefs), "row", axis=0, tiled=True
    )
    split = 2 * coefs
    across = lax.all_to_all(
        jnp.concatenate([active, proj[..., split:]], axis=-1), "col", 0, 1, tiled=True
    )
    across = swap(across)
    act_down, act_across = active, across[..., :width]
    pair = lambda values: jnp.stack([values[..., :coefs], values[..., coefs:]], axis=0)
    proj_down, proj_across = pair(proj[..., :split]), pair(across[..., width:])

    lanes = -(-width // LANES) * LANES
    lines = cols
    dtw = pad_to(pad_to(mine(dt_weight), 2, lanes), 1, coefs)
    dtwt = jnp.swapaxes(dtw, 1, 2)
    bias = jnp.broadcast_to(pad_to(mine(dt_bias), 1, lanes)[:, None, :], (dirs, 8, lanes))
    rates = -LOG2E * pad_to(mine(decay_rate), 2, lanes, 1.0)
    skip = jnp.broadcast_to(pad_to(mine(skip_gain), 1, lanes)[:, None, :], (dirs, 8, lanes))

    def params(at, count):
        wide = jnp.broadcast_to(rates[at : at + 2][:, :, None, :], (2, states, count, lanes))
        cut = slice(at, at + 2)
        return dtw[cut], dtwt[cut], bias[cut], wide, skip[cut], rank, states

    params_down, params_across = params(0, act_down.shape[1]), params(2, act_across.shape[1])
    act_down, act_across = pad_to(act_down, 2, lanes), pad_to(act_across, 2, lanes)
    y_down, start_down = run_forward(act_down, proj_down, params_down)
    y_across, start_across = run_forward(act_across, proj_across, params_across)
    y_back = lax.all_to_all(swap(y_across[..., :width].astype(BF16)), "col", 1, 0, tiled=True)
    summed = y_down[..., :width] + y_back.astype(F32)

    back_mixed = lax.dot_general(
        grad_all.reshape(-1, c_dim),
        lax.dynamic_slice_in_dim(out_full, me * width, width, axis=0),
        (((1,), (1,)), ((), ())),
        preferred_element_type=F32,
    ).reshape(all_rows, cols, width)
    gain = mine(norm_gain)
    sig = jax.nn.sigmoid(gate)
    silu = gate * sig
    back_norm = back_mixed * silu * gain
    own_mean = jnp.mean(summed, axis=-1)
    shifted = summed - own_mean[..., None]
    stats = jnp.stack(
        [own_mean, jnp.sum(shifted * shifted, -1), jnp.sum(back_norm, -1), jnp.sum(back_norm * shifted, -1)]
    )
    stats = lax.all_gather(stats, "row", axis=0)
    means = stats[:, 0]
    centre = jnp.mean(means, axis=0)
    off = means - centre
    variance = (jnp.sum(stats[:, 1], 0) + width * jnp.sum(off * off, 0)) / e_dim
    scale = lax.rsqrt(variance + NORM_EPS)
    flat_mean = jnp.sum(stats[:, 2], 0) / e_dim
    tilt_mean = scale * jnp.sum(stats[:, 3] + off * stats[:, 2], 0) / e_dim
    hat = (summed - centre[..., None]) * scale[..., None]
    normed = hat * gain
    mixed = (normed * silu).astype(BF16)
    back_gate = back_mixed * normed * (sig * (1.0 + gate * (1.0 - sig)))
    back_summed = scale[..., None] * (back_norm - flat_mean[..., None] - hat * tilt_mean[..., None])
    back_bf = back_summed.astype(BF16)
    gy_across = swap(lax.all_to_all(back_bf, "col", 0, 1, tiled=True))

    spots = jnp.repeat(jnp.arange(2 * states) + rank, lanes)
    pick = (spots[:, None] == jnp.arange(coefs)[None, :]).astype(BF16)
    dact_across, dproj_across = run_backward(
        act_across, proj_across, params_across, start_across, pad_to(gy_across, 2, lanes), pick
    )
    dact_down, dproj_down = run_backward(
        act_down, proj_down, params_down, start_down, pad_to(back_bf, 2, lanes), pick
    )
    unpair = lambda values: jnp.concatenate([values[0], values[1]], axis=-1)
    returned = lax.all_to_all(
        swap(jnp.concatenate([dact_across[..., :width], unpair(dproj_across)], axis=-1).astype(BF16)),
        "col", 1, 0, tiled=True,
    )
    dproj = jnp.concatenate([unpair(dproj_down), returned[..., width:].astype(F32)], axis=-1)
    dproj = lax.psum_scatter(dproj, "row", scatter_dimension=0, tiled=True)
    dproj = lax.all_gather(dproj.astype(BF16), "row", axis=0, tiled=True)
    proj_rows = lax.dynamic_slice_in_dim(proj_weight, me * width, width, axis=0)
    back_active = lax.dot_general(
        dproj.reshape(-1, dirs * coefs), proj_rows, (((1,), (1,)), ((), ())), preferred_element_type=F32
    ).reshape(all_rows, cols, width)
    back_active = back_active + dact_down[..., :width] + returned[..., :width].astype(F32)
    conv_sig = jax.nn.sigmoid(convolved)
    back_conv = back_active * (conv_sig * (1.0 + convolved * (1.0 - conv_sig)))
    grad_padded = col_halo(back_conv)
    back_source = jnp.zeros(source.shape, F32)
    for a in range(3):
        for b in range(3):
            back_source = back_source + grad_padded[2 - a : 2 - a + all_rows, 2 - b : 2 - b + cols] * taps[a, b]
    back_xz = jnp.concatenate([back_source.astype(BF16), back_gate.astype(BF16)], axis=-1)

    mixed_cells = lax.all_to_all(mixed, "row", 0, 2, tiled=True).reshape(-1, e_dim)
    result = field.astype(F32) + jnp.dot(mixed_cells, out_full, preferred_element_type=F32).reshape(field.shape)
    xz_cells = lax.all_to_all(back_xz, "row", 0, 2, tiled=True).reshape(-1, 2 * e_dim)
    grad_field = grad_out.astype(F32) + lax.dot_general(
        xz_cells, w_perm, (((1,), (1,)), ((), ())), preferred_element_type=F32
    ).reshape(field.shape)
    contract = (((0,), (0,)), ((), ()))
    in_part = lax.dot_general(
        field_flat, back_xz.reshape(-1, 2 * width), contract, preferred_element_type=F32
    )
    in_sum = lax.psum(in_part, "col")
    g_src, g_gate = in_sum[:, :width], in_sum[:, width:]
    back_one = lax.ppermute(jnp.where(even, g_src, g_gate), "row", reverse_moves(moves_one))
    back_two = lax.ppermute(jnp.where(even, g_gate, g_src), "row", reverse_moves(moves_two))
    grad_in = jnp.concatenate(
        [jnp.where(low, back_one, back_two), jnp.where(low, back_two, back_one)], axis=1
    )
    out_part = lax.dot_general(
        mixed.reshape(-1, width), grad_all.reshape(-1, c_dim), contract, preferred_element_type=F32
    )
    out_sum = lax.psum_scatter(out_part, "col", scatter_dimension=0, tiled=True)
    out_rows = lax.all_gather(out_sum, "row", axis=0)
    grad_out_w = lax.all_to_all(out_rows, "col", 0, 1, tiled=True).reshape(e_dim // nc, c_dim)
    return (result.astype(BF16), grad_field, grad_in, grad_out_w)


def solution(mesh):
    in_specs = (
        P("row", "col", None), P(None, "row"), P(), P(), P(), P(), P(), P(), P(), P("col", None), P("row", "col", None),
    )
    out_specs = (P("row", "col", None), P("row", "col", None), P(None, "row"), P("col", None))
    return jax.shard_map(local, mesh=mesh, in_specs=in_specs, out_specs=out_specs, check_vma=False)
```

profile of v0, /device:TPU:0, one launch (start us, length us, event | category | flops | bytes accessed | tf_op | source)
XLA Modules:
  0.0 471.4 jit_solution(2916443171711917022)
XLA Ops:
  10.4 4.4 collective-permute-start.1
  19.0 17.2 %all-gather.7.cloned.1.call-done = bf16[64,16,512]{2,1,0:T(8,128)(2,1)} async-done(((bf16[8,16,512]{2,1,0:T(8,128)(2,1)}), bf16[64,16,512]{2,1,0:T(8,128)(2,1)}) %all-gather.7.cloned.1.call-update) | async-done | bytes 1048592 | tf_op jit(solution)/shard_map/all_gather | solution.py:306
  43.1 4.1 collective-permute-done.2
  53.5 6.2 %all-to-all-done = bf16[64,16,128]{2,1,0:T(8,128)(2,1)S(1)} async-done(((bf16[64,16,128]{2,1,0:T(8,128)(2,1)}), bf16[64,16,128]{2,1,0:T(8,128)(2,1)S(1)}, u32[]{:S(2)}, u32[]{:S(2)}) %all-to-all-start) | async-done | bytes 262176 | tf_op jit(solution)/shard_map/all_to_all | solution.py:328
  60.1 8.9 %all_gather.31 = bf16[64,16,256]{2,1,0:T(8,128)(2,1)S(1)} all-gather(bf16[8,16,256]{2,1,0:T(8,128)(2,1)S(1)} %bitcast.179), channel_id=1, replica_groups=mesh['row'=8,'col'=4] {'row'}, dimensions={0}, use_global_device_ids=true | all-gather | bytes 589824 | tf_op jit(solution)/shard_map/all_gather | solution.py:330
  77.4 12.2 %all-to-all-done.1 = bf16[64,16,256]{2,1,0:T(8,128)(2,1)S(1)} async-done(((bf16[64,16,256]{2,1,0:T(8,128)(2,1)}), bf16[64,16,256]{2,1,0:T(8,128)(2,1)S(1)}, u32[]{:S(2)}, u32[]{:S(2)}) %all-to-all-start.1) | async-done | bytes 524320 | tf_op jit(solution)/shard_map/all_to_all | solution.py:334
  90.2 31.1 %scan_forward.3 = (f32[64,16,128]{2,1,0:T(8,128)S(1)}, f32[2,16,16,128]{3,2,1,0:T(8,128)S(1)}) custom-call(bf16[64,16,128]{2,1,0:T(8,128)(2,1)S(1)} %slice.321.refs_0_, bf16[2,64,16,64]{3,2,1,0:T(8,128)(2,1)S(1)} %pad_maximum_fusion.9.refs_1_, bf16[2,64,128]{2,1,0:T(8,128)(2,1)S(1)} %copy.85.refs_2_, f32[2,8,128]{2,1,0:T(8,128)S(1)} %broadcast_in_dim.19.refs_3_.refs_4_, ...), custom_call_target="tpu_custom_call" | custom-call | flops 83886080 | bytes 2097152 | tf_op jit(solution)/shard_map/scan_forward/pallas_call | solution.py:193
  122.1 4.0 all-to-all-start.2
  128.6 32.2 %scan_forward.2 = (f32[64,16,128]{2,1,0:T(8,128)S(1)}, f32[2,16,16,128]{3,2,1,0:T(8,128)S(1)}) custom-call(bf16[64,16,128]{2,1,0:T(8,128)(2,1)} %get-tuple-element.31.refs_0_, bf16[2,64,16,64]{3,2,1,0:T(8,128)(2,1)S(1)} %pad_maximum_fusion.7.refs_1_, bf16[2,64,128]{2,1,0:T(8,128)(2,1)S(1)} %copy.83.refs_2_, ...), custom_call_target="tpu_custom_call" | custom-call | flops 83886080 | bytes 2097152 | tf_op jit(solution)/shard_map/scan_forward/pallas_call | solution.py:193
  163.2 9.3 %all-gather = f32[32,64,16]{1,2,0:T(8,128)S(1)} all-gather(f32[4,64,16]{1,2,0:T(8,128)S(1)} %pad_maximum_fusion.19), channel_id=2, replica_groups=mesh['row'=8,'col'=4] {'row'}, dimensions={0}, use_global_device_ids=true | all-gather | bytes 147456 | tf_op jit(solution)/shard_map/all_gather | solution.py:377
  174.4 5.0 %all-to-all-start.4 = ((bf16[64,16,128]{2,1,0:T(8,128)(2,1)}), bf16[64,16,128]{2,1,0:T(8,128)(2,1)S(1)}, u32[]{:S(2)}, u32[]{:S(2)}) async-start(bf16[64,16,128]{2,1,0:T(8,128)(2,1)} %get-tuple-element.33.refs_8_), calls=%async_computation.4 | async-start | bytes 524288 | tf_op jit(solution)/shard_map/all_to_all | solution.py:391
  182.8 6.0 %all-to-all-done.4 = bf16[64,16,128]{2,1,0:T(8,128)(2,1)S(1)} async-done(((bf16[64,16,128]{2,1,0:T(8,128)(2,1)}), bf16[64,16,128]{2,1,0:T(8,128)(2,1)S(1)}, u32[]{:S(2)}, u32[]{:S(2)}) %all-to-all-start.4) | async-done | bytes 262176 | tf_op jit(solution)/shard_map/all_to_all | solution.py:391
  189.5 54.4 %scan_backward.3 = (f32[64,16,128]{2,1,0:T(8,128)}, f32[2,64,16,64]{3,2,1,0:T(8,128)}) custom-call(bf16[64,16,128]{2,1,0:T(8,128)(2,1)} %copy-done.3, bf16[2,64,16,64]{3,2,1,0:T(8,128)(2,1)} %copy-done.2, bf16[2,64,128]{2,1,0:T(8,128)(2,1)} %copy-done.7, bf16[2,128,64]{2,1,0:T(8,128)(2,1)} %get-tuple-element.60.refs_3_, f32[2,8,128]{2,1,0:T(8,128)} %copy-done.9, ...), custom_call_target="tpu_custom_call" | custom-call | flops 125829120 | bytes 4194304 | tf_op jit(solution)/shard_map/scan_backward/pallas_call | solution.py:221
  250.1 54.5 %scan_backward.2 = (f32[64,16,128]{2,1,0:T(8,128)}, f32[2,64,16,64]{3,2,1,0:T(8,128)}) custom-call(bf16[64,16,128]{2,1,0:T(8,128)(2,1)} %get-tuple-element.31.refs_0_, bf16[2,64,16,64]{3,2,1,0:T(8,128)(2,1)} %copy-done.1, bf16[2,64,128]{2,1,0:T(8,128)(2,1)} %copy-done.6, bf16[2,128,64]{2,1,0:T(8,128)(2,1)} %get-tuple-element.61.refs_3_, ...), custom_call_target="tpu_custom_call" | custom-call | flops 125829120 | bytes 4194304 | tf_op jit(solution)/shard_map/scan_backward/pallas_call | solution.py:221
  307.4 36.3 %reduce-scatter.3.cloned.1.call-done = f32[8,16,256]{2,1,0:T(8,128)} async-done(((f32[64,16,256]{2,1,0:T(8,128)}), f32[8,16,256]{2,1,0:T(8,128)}) %reduce-scatter.3.cloned.1.call-update) | async-done | bytes 131088 | tf_op jit(solution)/shard_map/reduce_scatter | solution.py:407
  344.7 9.9 %all_gather.36 = bf16[64,16,256]{2,1,0:T(8,128)(2,1)S(1)} all-gather(bf16[8,16,256]{2,1,0:T(8,128)(2,1)S(1)} %convert_element_type.121), channel_id=1, replica_groups=mesh['row'=8,'col'=4] {'row'}, dimensions={0}, use_global_device_ids=true | all-gather | bytes 589824 | tf_op jit(solution)/shard_map/all_gather | solution.py:408
  361.7 3.6 collective-permute-done.4
  368.9 3.6 all-to-all-start.3
  372.5 9.4 %reduce-scatter.5.cloned.1.call-done = f32[32,512]{1,0:T(8,128)} async-done(((f32[128,512]{1,0:T(8,128)}), f32[32,512]{1,0:T(8,128)}) %reduce-scatter.5.cloned.1.call-update) | async-done | bytes 65552 | tf_op jit(solution)/shard_map/reduce_scatter | solution.py:443
  381.9 11.8 %all-gather.1 = f32[256,512]{1,0:T(8,128)} all-gather(f32[32,512]{1,0:T(8,128)} %reduce-scatter.5.cloned.1.call-done), channel_id=3, replica_groups=mesh['row'=8,'col'=4] {'row'}, dimensions={0}, use_global_device_ids=true | all-gather | bytes 589824 | tf_op jit(solution)/shard_map/all_gather | solution.py:444
  398.1 15.0 %all-to-all-done.7 = f32[8,32,512]{2,1,0:T(8,128)S(1)} async-done(((f32[8,32,512]{2,1,0:T(8,128)}), f32[8,32,512]{2,1,0:T(8,128)S(1)}, u32[]{:S(2)}, u32[]{:S(2)}) %all-to-all-start.7) | async-done | bytes 524320 | tf_op jit(solution)/shard_map/all_to_all | solution.py:445
  413.1 3.5 all-to-all-start.6
  418.4 7.8 %all-to-all-done.6 = bf16[64,16,256]{2,1,0:T(8,128)(2,1)S(1)} async-done(((bf16[64,16,256]{2,1,0:T(8,128)(2,1)}), bf16[64,16,256]{2,1,0:T(8,128)(2,1)S(1)}, u32[]{:S(2)}, u32[]{:S(2)}) %all-to-all-start.6) | async-done | bytes 524320 | tf_op jit(solution)/shard_map/all_to_all | solution.py:425
  431.4 29.2 %all-gather.13.cloned.1.call-done = bf16[512,2048]{1,0:T(8,128)(2,1)} async-done(((bf16[512,256]{1,0:T(8,128)(2,1)}), bf16[512,2048]{1,0:T(8,128)(2,1)}) %all-gather.13.cloned.1.call-update) | async-done | bytes 2097168 | tf_op jit(solution)/shard_map/all_gather | solution.py:318
  (210 shorter events, 76.6 us)
Async XLA Ops:
  7.2 28.9 %all-gather.7.cloned.1.call-start = ((), (), s32[]{:S(2)}) async-start(), calls=%async_computation.10 | async-start | bytes 1179648 | tf_op jit(solution)/shard_map/all_gather | solution.py:306
  7.9 118.3 %all-gather.9.cloned.1.call-start = ((), (), s32[]{:S(2)}) async-start(), calls=%async_computation.11 | async-start | bytes 1310720 | tf_op jit(solution)/shard_map/all_gather | solution.py:317
  8.7 117.6 %all-gather.11.cloned.1.call-start = ((), (), s32[]{:S(2)}) async-start(), calls=%async_computation.12 | async-start | bytes 1179648 | tf_op jit(solution)/shard_map/all_gather | solution.py:316
  9.7 6.0 %collective-permute-start = (bf16[512,128]{1,0:T(8,128)(2,1)S(1)}, bf16[512,128]{1,0:T(8,128)(2,1)S(1)}, u32[]{:S(2)}, u32[]{:S(2)}) collective-permute-start(bf16[512,128]{1,0:T(8,128)(2,1)S(1)} %get-tuple-element.58), channel_id=1, source_target_pairs={{0,0},{4,8},{8,16},{12,24},{16,4},{20,12},{24,20},{28,28},{1,1},{5... | collective-permute-start | bytes 393224 | tf_op jit(solution)/shard_map/ppermute | solution.py:308
  10.4 8.5 %collective-permute-start.1 = (bf16[512,128]{1,0:T(8,128)(2,1)S(1)}, bf16[512,128]{1,0:T(8,128)(2,1)S(1)}, u32[]{:S(2)}, u32[]{:S(2)}) collective-permute-start(bf16[512,128]{1,0:T(8,128)(2,1)S(1)} %get-tuple-element.59), channel_id=1, source_target_pairs={{0,4},{4,12},{8,20},{12,28},{16,0},{20,8},{24,16},{28,24},{1,5},{5... | collective-permute-start | bytes 393224 | tf_op jit(solution)/shard_map/ppermute | solution.py:309
  38.1 5.0 %collective-permute-start.3 = (bf16[64,1,128]{2,1,0:T(2,128)(2,1)S(1)}, bf16[64,1,128]{2,1,0:T(2,128)(2,1)S(1)}, u32[]{:S(2)}, u32[]{:S(2)}) collective-permute-start(bf16[64,1,128]{2,1,0:T(2,128)(2,1)S(1)} %get-tuple-element.53), channel_id=1, source_target_pairs={{1,0},{2,1},{3,2},{0,3},{5,4},{6,5},{7,6},{4,7},{9,8},{10,9},{11,1... | collective-permute-start | bytes 49160 | tf_op jit(solution)/shard_map/ppermute | solution.py:284
  41.5 5.7 %collective-permute-start.2 = (bf16[64,1,128]{2,1,0:T(2,128)(2,1)S(1)}, bf16[64,1,128]{2,1,0:T(2,128)(2,1)S(1)}, u32[]{:S(2)}, u32[]{:S(2)}) collective-permute-start(bf16[64,1,128]{2,1,0:T(2,128)(2,1)S(1)} %get-tuple-element.52), channel_id=1, source_target_pairs={{0,1},{1,2},{2,3},{3,0},{4,5},{5,6},{6,7},{7,4},{8,9},{9,10},{10,1... | collective-permute-start | bytes 49160 | tf_op jit(solution)/shard_map/ppermute | solution.py:283
  49.4 10.3 %all-to-all-start = ((bf16[64,16,128]{2,1,0:T(8,128)(2,1)}), bf16[64,16,128]{2,1,0:T(8,128)(2,1)S(1)}, u32[]{:S(2)}, u32[]{:S(2)}) async-start(bf16[64,16,128]{2,1,0:T(8,128)(2,1)} %get-tuple-element.31.refs_0_), calls=%async_computation | async-start | bytes 524288 | tf_op jit(solution)/shard_map/all_to_all | solution.py:328
  70.8 18.7 %all-to-all-start.1 = ((bf16[64,16,256]{2,1,0:T(8,128)(2,1)}), bf16[64,16,256]{2,1,0:T(8,128)(2,1)S(1)}, u32[]{:S(2)}, u32[]{:S(2)}) async-start(bf16[64,16,256]{2,1,0:T(8,128)(2,1)} %pad_maximum_fusion.8), calls=%async_computation.1 | async-start | bytes 1048576 | tf_op jit(solution)/shard_map/all_to_all | solution.py:334
  75.2 53.4 %copy-start.6 = (bf16[2,64,128]{2,1,0:T(8,128)(2,1)}, bf16[2,64,128]{2,1,0:T(8,128)(2,1)S(1)}, u32[]{:S(2)}) copy-start(bf16[2,64,128]{2,1,0:T(8,128)(2,1)S(1)} %copy.83.refs_2_) | copy-start | bytes 98308
  122.1 38.8 %all-to-all-start.2 = ((bf16[16,64,128]{2,0,1:T(8,128)(2,1)}), bf16[16,64,128]{2,0,1:T(8,128)(2,1)}, u32[]{:S(2)}, u32[]{:S(2)}) async-start(bf16[16,64,128]{2,0,1:T(8,128)(2,1)} %convert_bitcast_fusion), calls=%async_computation.2 | async-start | bytes 524288 | tf_op jit(solution)/shard_map/all_to_all | solution.py:359
  174.4 14.4 %all-to-all-start.4 = ((bf16[64,16,128]{2,1,0:T(8,128)(2,1)}), bf16[64,16,128]{2,1,0:T(8,128)(2,1)S(1)}, u32[]{:S(2)}, u32[]{:S(2)}) async-start(bf16[64,16,128]{2,1,0:T(8,128)(2,1)} %get-tuple-element.33.refs_8_), calls=%async_computation.4 | async-start | bytes 524288 | tf_op jit(solution)/shard_map/all_to_all | solution.py:391
  246.4 59.4 %all-to-all-start.5 = ((bf16[16,64,256]{2,0,1:T(8,128)(2,1)}), bf16[16,64,256]{2,0,1:T(8,128)(2,1)S(1)}, u32[]{:S(2)}, u32[]{:S(2)}) async-start(bf16[16,64,256]{2,0,1:T(8,128)(2,1)} %maximum_bitcast_fusion), calls=%async_computation.5 | async-start | bytes 1048576 | tf_op jit(solution)/shard_map/all_to_all | solution.py:402
  249.8 93.9 %reduce-scatter.3.cloned.1.call-start = ((), (), s32[]{:S(2)}) async-start(), calls=%async_computation.13 | async-start | bytes 1179648 | tf_op jit(solution)/shard_map/reduce_scatter | solution.py:407
  307.4 74.5 %reduce-scatter.5.cloned.1.call-start = ((), (), s32[]{:S(2)}) async-start(), calls=%async_computation.16 | async-start | bytes 327680 | tf_op jit(solution)/shard_map/reduce_scatter | solution.py:443
  356.3 5.5 %collective-permute-start.5 = (f32[64,1,128]{2,1,0:T(1,128)S(1)}, f32[64,1,128]{2,1,0:T(1,128)S(1)}, u32[]{:S(2)}, u32[]{:S(2)}) collective-permute-start(f32[64,1,128]{2,1,0:T(1,128)S(1)} %get-tuple-element.45), channel_id=1, source_target_pairs={{1,0},{2,1},{3,2},{0,3},{5,4},{6,5},{7,6},{4,7},{9,8},{10,9},{11,1... | collective-permute-start | bytes 98312 | tf_op jit(solution)/shard_map/ppermute | solution.py:284
  359.6 5.7 %collective-permute-start.4 = (f32[64,1,128]{2,1,0:T(1,128)S(1)}, f32[64,1,128]{2,1,0:T(1,128)S(1)}, u32[]{:S(2)}, u32[]{:S(2)}) collective-permute-start(f32[64,1,128]{2,1,0:T(1,128)S(1)} %get-tuple-element.44), channel_id=1, source_target_pairs={{0,1},{1,2},{2,3},{3,0},{4,5},{5,6},{6,7},{7,4},{8,9},{9,10},{10,1... | collective-permute-start | bytes 98312 | tf_op jit(solution)/shard_map/ppermute | solution.py:283
  361.7 64.6 %all-reduce.3.cloned.1.call-start = ((), (), s32[]{:S(2)}) async-start(), calls=%async_computation.15 | async-start | bytes 1048576 | tf_op jit(solution)/shard_map/psum | solution.py:433
  368.1 92.5 %all-gather.13.cloned.1.call-start = ((), (), s32[]{:S(2)}) async-start(), calls=%async_computation.14 | async-start | bytes 2359296 | tf_op jit(solution)/shard_map/all_gather | solution.py:318
  368.9 24.8 %all-to-all-start.3 = ((bf16[64,16,128]{2,1,0:T(8,128)(2,1)}), bf16[64,16,128]{2,1,0:T(8,128)(2,1)S(1)}, u32[]{:S(2)}, u32[]{:S(2)}) async-start(bf16[64,16,128]{2,1,0:T(8,128)(2,1)} %get-tuple-element.35), calls=%async_computation.3 | async-start | bytes 524288 | tf_op jit(solution)/shard_map/all_to_all | solution.py:423
  393.7 19.3 %all-to-all-start.7 = ((f32[8,32,512]{2,1,0:T(8,128)}), f32[8,32,512]{2,1,0:T(8,128)S(1)}, u32[]{:S(2)}, u32[]{:S(2)}) async-start(f32[8,32,512]{2,1,0:T(8,128)} %bitcast.64), calls=%async_computation.9 | async-start | bytes 1048576 | tf_op jit(solution)/shard_map/all_to_all | solution.py:445
  413.1 13.2 %all-to-all-start.6 = ((bf16[64,16,256]{2,1,0:T(8,128)(2,1)}), bf16[64,16,256]{2,1,0:T(8,128)(2,1)S(1)}, u32[]{:S(2)}, u32[]{:S(2)}) async-start(bf16[64,16,256]{2,1,0:T(8,128)(2,1)} %pad_maximum_fusion.10), calls=%async_computation.7 | async-start | bytes 1048576 | tf_op jit(solution)/shard_map/all_to_all | solution.py:425
  427.4 36.3 %collective-permute-start.6 = (f32[512,128]{1,0:T(8,128)S(1)}, f32[512,128]{1,0:T(8,128)S(1)}, u32[]{:S(2)}, u32[]{:S(2)}) collective-permute-start(f32[512,128]{1,0:T(8,128)S(1)} %get-tuple-element.42), channel_id=1, source_target_pairs={{0,0},{8,4},{16,8},{24,12},{4,16},{12,20},{20,24},{28,28},{1,1},{9... | collective-permute-start | bytes 786440 | tf_op jit(solution)/shard_map/ppermute | solution.py:435
  428.1 35.6 %collective-permute-start.7 = (f32[512,128]{1,0:T(8,128)S(1)}, f32[512,128]{1,0:T(8,128)S(1)}, u32[]{:S(2)}, u32[]{:S(2)}) collective-permute-start(f32[512,128]{1,0:T(8,128)S(1)} %get-tuple-element.43), channel_id=1, source_target_pairs={{4,0},{12,4},{20,8},{28,12},{0,16},{8,20},{16,24},{24,28},{5,1},{1... | collective-permute-start | bytes 786440 | tf_op jit(solution)/shard_map/ppermute | solution.py:436
  (41 other events, 736.4 us)
Sparse Core Ops, SparseCore 0:
  9.9 26.1 all-gather.6
  37.7 27.9 all-gather.8
  67.5 23.0 all-gather.10
  307.5 36.2 reduce-scatter.2
  361.8 20.0 reduce-scatter.4
  384.2 38.9 all-reduce.2
  425.8 34.6 all-gather.12
where the time goes:
time: 473 us; the launch traced here: 471 us
  Pallas kernels  172 us (36%)
  waiting for transfers between devices  152 us (32%)
  starting transfers between devices  46.2 us (10%)
  blocking collectives  40 us (8%)
  other arithmetic  20.6 us (4%)
  between operations  15.2 us (3%)
  matrix products  12.7 us (3%)
  local copies, waits for them, and re-layouts  12.3 us (3%)
    pallas_call x2, Pallas kernels, run_backward(): pl.pallas_call(lambda *refs: backward_kernel(rank, states, *refs), grid=(...  109 us
    pallas_call x2, Pallas kernels, run_forward(): pl.pallas_call(lambda *refs: forward_kernel(rank, states, *refs), grid=(2...  63.4 us
    reduce_scatter x1, waiting for transfers between devices, local(): dproj = lax.psum_scatter(dproj, 'row', scatter_dimension=0, tiled=True)  36.3 us
    all_gather x1, waiting for transfers between devices, local(): w_perm = lax.all_gather(w_mine, 'row', axis=1, tiled=True)  29.2 us
    all_gather x1, waiting for transfers between devices, local(): field_all = lax.all_gather(field, 'row', axis=0, tiled=True)  17.2 us
    all_to_all x1, waiting for transfers between devices, local(): lax.all_to_all(out_rows, 'col', 0, 1, tiled=True)  15 us
    all_to_all x1, waiting for transfers between devices, local(): lax.all_to_all(jnp.concatenate([active, proj[..., split:]], axis=-1), 'co...  12.2 us
    all_gather x1, blocking collectives, local(): out_rows = lax.all_gather(out_sum, 'row', axis=0)  11.8 us
  transfers between devices with their start and end apart: 23, of which 13 were waited for; matrix products, arithmetic and copies ran while one was open for 7% of the time, Pallas kernels for 25%

commit v1 on v0

--- a/solution.py
+++ b/solution.py
@@ -34,32 +34,55 @@
         step_ref[pl.ds(c * chunk, chunk)] = DT_FLOOR + softplus(raw)
 
 
-def column(values, i, like):
-    return jnp.broadcast_to(values[:, i : i + 1], like.shape)
-
-
-def forward_kernel(rank, states, act_ref, proj_ref, dtw_ref, bias_ref, rate_ref, skip_ref, y_ref, start_ref, step_ref):
+def spread_coefs(proj_ref, spread_ref, wide_ref):
+    length, lines, coefs = proj_ref.shape
+    chunk = 16
+
+    @pl.loop(0, length // chunk)
+    def _(c):
+        at = pl.ds(c * chunk, chunk)
+        rows = proj_ref[at].reshape(chunk * lines, coefs)
+        for n in range(wide_ref.shape[-1] // 512):
+            cut = pl.ds(n * 512, 512)
+            out = jnp.dot(rows, spread_ref[:, cut], preferred_element_type=F32)
+            wide_ref[at, :, cut] = out.reshape(chunk, lines, 512)
+
+
+def loop(count, body, carry, unroll):
+    def several(i, carry):
+        for j in range(unroll):
+            carry = body(i * unroll + j, carry)
+        return carry
+
+    return lax.fori_loop(0, count // unroll, several, carry)
+
+
+def forward_kernel(
+    states, act_ref, proj_ref, dtw_ref, bias_ref, rate_ref, skip_ref, spread_ref, y_ref, start_ref, step_ref, wide_ref,
+):
     k = pl.program_id(0)
     length, lines, width = act_ref.shape
     fill_steps(proj_ref, dtw_ref, bias_ref, None, step_ref)
+    spread_coefs(proj_ref, spread_ref, wide_ref)
     zero = jnp.zeros((lines, width), F32)
 
     def place(i):
         return jnp.where(k == 0, i, length - 1 - i)
+
+    def coef(p, n):
+        return wide_ref[p, :, pl.ds(n * width, width)]
 
     def first(i, carry):
         state, total = carry
         p = place(i)
         step = step_ref[p]
         drive = step * act_ref[p].astype(F32)
-        coef = proj_ref[p].astype(F32)
         state = tuple(
-            jnp.exp2(step * rate_ref[n]) * state[n] + drive * column(coef, rank + n, step)
-            for n in range(states)
+            jnp.exp2(step * rate_ref[n]) * state[n] + drive * coef(p, n) for n in range(states)
         )
         return state, total + step
 
-    state, total = lax.fori_loop(0, length, first, ((zero,) * states, zero))
+    state, total = loop(length, first, ((zero,) * states, zero), 2)
     closed = []
     for n in range(states):
         one = state[n] / (1.0 - jnp.exp2(total * rate_ref[n]))
@@ -77,61 +100,60 @@
         step = step_ref[p]
         act = act_ref[p].astype(F32)
         drive = step * act
-        coef = proj_ref[p].astype(F32)
         y = y_ref[p] + skip * act
         new = []
         for n in range(states):
-            one = jnp.exp2(step * rate_ref[n]) * state[n] + drive * column(coef, rank + n, step)
-            y = y + one * column(coef, rank + states + n, step)
+            one = jnp.exp2(step * rate_ref[n]) * state[n] + drive * coef(p, n)
+            y = y + one * coef(p, states + n)
             new.append(one)
         y_ref[p] = y
         return tuple(new)
 
-    lax.fori_loop(0, length, second, tuple(closed))
+    loop(length, second, tuple(closed), 2)
 
 
 def backward_kernel(
-    rank, states, act_ref, proj_ref, dtw_ref, dtwt_ref, bias_ref, rate_ref, skip_ref, start_ref, gy_ref, pick_ref,
-    dact_ref, dproj_ref, raw_ref, step_ref, h_ref, a_ref, prod_ref, draw_ref,
+    states, act_ref, proj_ref, dtw_ref, dtwt_ref, bias_ref, rate_ref, skip_ref, start_ref, gy_ref, pick_ref, spread_ref,
+    dact_ref, dproj_ref, raw_ref, step_ref, h_ref, wide_ref, prod_ref, draw_ref,
 ):
     k = pl.program_id(0)
     length, lines, width = act_ref.shape
     fill_steps(proj_ref, dtw_ref, bias_ref, raw_ref, step_ref)
+    spread_coefs(proj_ref, spread_ref, wide_ref)
     zero = jnp.zeros((lines, width), F32)
 
     def place(i):
         return jnp.where(k == 0, i, length - 1 - i)
 
+    def coef(p, n):
+        return wide_ref[p, :, pl.ds(n * width, width)]
+
     for n in range(states):
-        h_ref[0, n] = start_ref[n]
+        h_ref[0, n] = start_ref[n].astype(BF16)
 
     def replay(i, carry):
         state, total = carry
         p = place(i)
         step = step_ref[p]
         drive = step * act_ref[p].astype(F32)
-        coef = proj_ref[p].astype(F32)
         new = []
         for n in range(states):
-            decay = jnp.exp2(step * rate_ref[n])
-            one = decay * state[n] + drive * column(coef, rank + n, step)
-            a_ref[i, n] = decay
-            h_ref[i + 1, n] = one
+            one = jnp.exp2(step * rate_ref[n]) * state[n] + drive * coef(p, n)
+            h_ref[i + 1, n] = one.astype(BF16)
             new.append(one)
         return tuple(new), total + step
 
-    _, total = lax.fori_loop(0, length, replay, (tuple(start_ref[n] for n in range(states)), zero))
+    _, total = loop(length, replay, (tuple(start_ref[n] for n in range(states)), zero), 2)
 
     def adjoint(j, back):
-        i = length - 1 - j
-        p = place(i)
+        p = place(length - 1 - j)
         gy = gy_ref[p].astype(F32)
-        coef = proj_ref[p].astype(F32)
+        step = step_ref[p]
         return tuple(
-            a_ref[i, n] * (back[n] + gy * column(coef, rank + states + n, gy)) for n in range(states)
+            jnp.exp2(step * rate_ref[n]) * (back[n] + gy * coef(p, states + n)) for n in range(states)
         )
 
-    back = lax.fori_loop(0, length, adjoint, (zero,) * states)
+    back = loop(length, adjoint, (zero,) * states, 2)
     back = tuple(back[n] / (1.0 - jnp.exp2(total * rate_ref[n])) for n in range(states))
 
     @pl.when(k == 0)
@@ -139,42 +161,46 @@
         dact_ref[...] = jnp.zeros_like(dact_ref)
 
     skip = jnp.broadcast_to(skip_ref[0:1, :], (lines, width))
-
-    def last(j, back):
-        i = length - 1 - j
-        p = place(i)
-        gy = gy_ref[p].astype(F32)
-        coef = proj_ref[p].astype(F32)
-        step = step_ref[p]
-        act = act_ref[p].astype(F32)
-        drive = step * act
-        ddrive = zero
-        dstep = zero
-        new = []
-        for n in range(states):
-            lam = back[n] + gy * column(coef, rank + states + n, gy)
-            prod_ref[p, :, pl.ds(n * width, width)] = (drive * lam).astype(BF16)
-            prod_ref[p, :, pl.ds((states + n) * width, width)] = (gy * h_ref[i + 1, n]).astype(BF16)
-            ddrive = ddrive + lam * column(coef, rank + n, gy)
-            carried = a_ref[i, n] * lam
-            dstep = dstep + (carried * h_ref[i, n]) * rate_ref[n]
-            new.append(carried)
-        dstep = LN2 * dstep + act * ddrive
-        dact_ref[p] = dact_ref[p] + step * ddrive + skip * gy
-        draw_ref[p] = (dstep / (1.0 + jnp.exp(-raw_ref[p]))).astype(BF16)
-        return tuple(new)
-
-    lax.fori_loop(0, length, last, back)
-    chunk = 8
-
-    @pl.loop(0, length // chunk)
-    def _(c):
-        at = pl.ds(c * chunk, chunk)
-        prods = prod_ref[at].reshape(chunk * lines, prod_ref.shape[-1])
-        raws = draw_ref[at].reshape(chunk * lines, width)
+    chunk = prod_ref.shape[0]
+
+    def part(c, back):
+        first_j = c * chunk
+
+        def last(q, back):
+            i = length - 1 - (first_j + q)
+            p = place(i)
+            gy = gy_ref[p].astype(F32)
+            step = step_ref[p]
+            act = act_ref[p].astype(F32)
+            drive = step * act
+            ddrive = zero
+            dstep = zero
+            new = []
+            for n in range(states):
+                rate = rate_ref[n]
+                lam = back[n] + gy * coef(p, states + n)
+                prod_ref[q, :, pl.ds(n * width, width)] = (drive * lam).astype(BF16)
+                prod_ref[q, :, pl.ds((states + n) * width, width)] = (gy * h_ref[i + 1, n].astype(F32)).astype(BF16)
+                ddrive = ddrive + lam * coef(p, n)
+                carried = jnp.exp2(step * rate) * lam
+                dstep = dstep + (carried * h_ref[i, n].astype(F32)) * rate
+                new.append(carried)
+            dstep = LN2 * dstep + act * ddrive
+            dact_ref[p] = dact_ref[p] + step * ddrive + skip * gy
+            draw_ref[q] = (dstep / (1.0 + jnp.exp(-raw_ref[p]))).astype(BF16)
+            return tuple(new)
+
+        back = loop(chunk, last, back, 2)
+        prods = prod_ref[...].reshape(chunk * lines, prod_ref.shape[-1])
+        raws = draw_ref[...].reshape(chunk * lines, width)
         out = jnp.dot(prods, pick_ref[...], preferred_element_type=F32)
         out = out + jnp.dot(raws, dtwt_ref[...], preferred_element_type=F32)
-        dproj_ref[at] = out.reshape(chunk, lines, out.shape[-1])
+        out = out.reshape(chunk, lines, out.shape[-1])
+        for q in range(chunk):
+            dproj_ref[place(length - 1 - (first_j + q))] = out[q]
+        return back
+
+    lax.fori_loop(0, length // chunk, part, back)
 
 
 def whole_spec(shape):
@@ -185,13 +211,13 @@
     return pl.BlockSpec((None,) + shape, lambda k: (k,) + (0,) * len(shape))
 
 
-def run_forward(act, proj, params):
+def run_forward(act, proj, params, spread):
     dtw, dtwt, bias, rates, skip, rank, states = params
     length, lines, width = act.shape
     coefs = proj.shape[-1]
     work = 2 * 2 * length * lines * width * states
     return pl.pallas_call(
-        lambda *refs: forward_kernel(rank, states, *refs),
+        lambda *refs: forward_kernel(states, *refs),
         grid=(2,),
         in_specs=[
             whole_spec(act.shape),
@@ -200,26 +226,30 @@
             each_spec((8, width)),
             each_spec((states, lines, width)),
             each_spec((8, width)),
+            whole_spec(spread.shape),
         ],
         out_specs=[whole_spec(act.shape), each_spec((states, lines, width))],
         out_shape=[
             jax.ShapeDtypeStruct(act.shape, F32),
             jax.ShapeDtypeStruct((2, states, lines, width), F32),
         ],
-        scratch_shapes=[pltpu.VMEM(act.shape, F32)],
-        compiler_params=pltpu.CompilerParams(vmem_limit_bytes=40 * 2**20),
+        scratch_shapes=[
+            pltpu.VMEM(act.shape, F32),
+            pltpu.VMEM((length, lines, 2 * states * width), F32),
+        ],
+        compiler_params=pltpu.CompilerParams(vmem_limit_bytes=56 * 2**20),
         cost_estimate=pl.CostEstimate(flops=10 * work, bytes_accessed=4 * act.size * 4, transcendentals=work),
         name="scan_forward",
-    )(act, proj, dtw, bias, rates, skip)
-
-
-def run_backward(act, proj, params, start, gy, pick):
+    )(act, proj, dtw, bias, rates, skip, spread)
+
+
+def run_backward(act, proj, params, start, gy, pick, spread):
     dtw, dtwt, bias, rates, skip, rank, states = params
     length, lines, width = act.shape
     coefs = proj.shape[-1]
     work = 2 * 3 * length * lines * width * states
     return pl.pallas_call(
-        lambda *refs: backward_kernel(rank, states, *refs),
+        lambda *refs: backward_kernel(states, *refs),
         grid=(2,),
         in_specs=[
             whole_spec(act.shape),
@@ -232,6 +262,7 @@
             each_spec((states, lines, width)),
             whole_spec(act.shape),
             whole_spec(pick.shape),
+            whole_spec(spread.shape),
         ],
         out_specs=[whole_spec(act.shape), each_spec((length, lines, coefs))],
         out_shape=[
@@ -241,15 +272,15 @@
         scratch_shapes=[
             pltpu.VMEM(act.shape, F32),
             pltpu.VMEM(act.shape, F32),
-            pltpu.VMEM((length + 1, states, lines, width), F32),
-            pltpu.VMEM((length, states, lines, width), F32),
-            pltpu.VMEM((length, lines, 2 * states * width), BF16),
-            pltpu.VMEM(act.shape, BF16),
+            pltpu.VMEM((length + 1, states, lines, width), BF16),
+            pltpu.VMEM((length, lines, 2 * states * width), F32),
+            pltpu.VMEM((8, lines, 2 * states * width), BF16),
+            pltpu.VMEM((8, lines, width), BF16),
         ],
         compiler_params=pltpu.CompilerParams(vmem_limit_bytes=60 * 2**20),
         cost_estimate=pl.CostEstimate(flops=10 * work, bytes_accessed=8 * act.size * 4, transcendentals=work),
         name="scan_backward",
-    )(act, proj, dtw, dtwt, bias, rates, skip, start, gy, pick)
+    )(act, proj, dtw, dtwt, bias, rates, skip, start, gy, pick, spread)
 
 
 def pad_to(values, axis, size, fill=0.0):
@@ -354,8 +385,11 @@
 
     params_down, params_across = params(0, act_down.shape[1]), params(2, act_across.shape[1])
     act_down, act_across = pad_to(act_down, 2, lanes), pad_to(act_across, 2, lanes)
-    y_down, start_down = run_forward(act_down, proj_down, params_down)
-    y_across, start_across = run_forward(act_across, proj_across, params_across)
+    spots = jnp.repeat(jnp.arange(2 * states) + rank, lanes)
+    pick = (spots[:, None] == jnp.arange(coefs)[None, :]).astype(BF16)
+    spread = pick.T
+    y_across, start_across = run_forward(act_across, proj_across, params_across, spread)
+    y_down, start_down = run_forward(act_down, proj_down, params_down, spread)
     y_back = lax.all_to_all(swap(y_across[..., :width].astype(BF16)), "col", 1, 0, tiled=True)
     summed = y_down[..., :width] + y_back.astype(F32)
 
@@ -390,21 +424,32 @@
     back_bf = back_summed.astype(BF16)
     gy_across = swap(lax.all_to_all(back_bf, "col", 0, 1, tiled=True))
 
-    spots = jnp.repeat(jnp.arange(2 * states) + rank, lanes)
-    pick = (spots[:, None] == jnp.arange(coefs)[None, :]).astype(BF16)
     dact_across, dproj_across = run_backward(
-        act_across, proj_across, params_across, start_across, pad_to(gy_across, 2, lanes), pick
-    )
+        act_across, proj_across, params_across, start_across, pad_to(gy_across, 2, lanes), pick, spread
+    )
+    contract = (((0,), (0,)), ((), ()))
+    mixed_cells = lax.all_to_all(mixed, "row", 0, 2, tiled=True).reshape(-1, e_dim)
+    out_part = lax.dot_general(
+        mixed.reshape(-1, width), grad_all.reshape(-1, c_dim), contract, preferred_element_type=F32
+    )
+    out_sum = lax.psum_scatter(out_part, "col", scatter_dimension=0, tiled=True)
+    out_rows = lax.all_gather(out_sum.astype(BF16), "row", axis=0)
+    back_bf, out_rows, mixed_cells, w_perm = lax.optimization_barrier((back_bf, out_rows, mixed_cells, w_perm))
+    grad_out_w = lax.all_to_all(out_rows, "col", 0, 1, tiled=True).reshape(e_dim // nc, c_dim)
     dact_down, dproj_down = run_backward(
-        act_down, proj_down, params_down, start_down, pad_to(back_bf, 2, lanes), pick
-    )
+        act_down, proj_down, params_down, start_down, pad_to(back_bf, 2, lanes), pick, spread
+    )
+    dproj_down, grad_out_w = lax.optimization_barrier((dproj_down, grad_out_w))
     unpair = lambda values: jnp.concatenate([values[0], values[1]], axis=-1)
     returned = lax.all_to_all(
         swap(jnp.concatenate([dact_across[..., :width], unpair(dproj_across)], axis=-1).astype(BF16)),
         "col", 1, 0, tiled=True,
     )
     dproj = jnp.concatenate([unpair(dproj_down), returned[..., width:].astype(F32)], axis=-1)
-    dproj = lax.psum_scatter(dproj, "row", scatter_dimension=0, tiled=True)
+    dproj = lax.all_to_all(
+        dproj.astype(BF16).reshape(nr, rows, cols, dirs * coefs), "row", 0, 0, tiled=True
+    )
+    dproj = jnp.sum(dproj.astype(F32), axis=0)
     dproj = lax.all_gather(dproj.astype(BF16), "row", axis=0, tiled=True)
     proj_rows = lax.dynamic_slice_in_dim(proj_weight, me * width, width, axis=0)
     back_active = lax.dot_general(
@@ -420,13 +465,11 @@
             back_source = back_source + grad_padded[2 - a : 2 - a + all_rows, 2 - b : 2 - b + cols] * taps[a, b]
     back_xz = jnp.concatenate([back_source.astype(BF16), back_gate.astype(BF16)], axis=-1)
 
-    mixed_cells = lax.all_to_all(mixed, "row", 0, 2, tiled=True).reshape(-1, e_dim)
     result = field.astype(F32) + jnp.dot(mixed_cells, out_full, preferred_element_type=F32).reshape(field.shape)
     xz_cells = lax.all_to_all(back_xz, "row", 0, 2, tiled=True).reshape(-1, 2 * e_dim)
     grad_field = grad_out.astype(F32) + lax.dot_general(
         xz_cells, w_perm, (((1,), (1,)), ((), ())), preferred_element_type=F32
     ).reshape(field.shape)
-    contract = (((0,), (0,)), ((), ()))
     in_part = lax.dot_general(
         field_flat, back_xz.reshape(-1, 2 * width), contract, preferred_element_type=F32
     )
@@ -437,13 +480,7 @@
     grad_in = jnp.concatenate(
         [jnp.where(low, back_one, back_two), jnp.where(low, back_two, back_one)], axis=1
     )
-    out_part = lax.dot_general(
-        mixed.reshape(-1, width), grad_all.reshape(-1, c_dim), contract, preferred_element_type=F32
-    )
-    out_sum = lax.psum_scatter(out_part, "col", scatter_dimension=0, tiled=True)
-    out_rows = lax.all_gather(out_sum, "row", axis=0)
-    grad_out_w = lax.all_to_all(out_rows, "col", 0, 1, tiled=True).reshape(e_dim // nc, c_dim)
-    return (result.astype(BF16), grad_field, grad_in, grad_out_w)
+    return (result.astype(BF16), grad_field, grad_in, grad_out_w.astype(F32))
 
 
 def solution(mesh):

time: 473 us -> 392 us (0.83)
  Pallas kernels: 172 us -> 105 us
  waiting for transfers between devices: 152 us -> 102 us
  blocking collectives: 40 us -> 59.4 us
  other arithmetic: 20.6 us -> 31.4 us
  local copies, waits for them, and re-layouts: 12.3 us -> 20.6 us
    pallas_call x4, Pallas kernels: 172 us -> 105 us  [the longest x2 69.7 us: run_backward(): pl.pallas_call(lambda *refs: backward_kernel(states, *refs), grid=(2,), i...]
    reduce_scatter x1 -> x0, waiting for transfers between devices: 36.3 us -> none  [local(): dproj = lax.psum_scatter(dproj, 'row', scatter_dimension=0, tiled=True)]
    all_to_all x0 -> x2, blocking collectives: none -> 21.8 us  [the longest x1 12.3 us: local(): lax.all_to_all(dproj.astype(BF16).reshape(nr, rows, cols, dirs * coefs),...]
    psum x1, waiting for transfers between devices: 0.02 us -> 20.8 us  [local(): in_sum = lax.psum(in_part, 'col')]
    all_to_all x1, waiting for transfers between devices: 15 us -> 0.01 us  [local(): lax.all_to_all(out_rows, 'col', 0, 1, tiled=True)]
    all_gather x1, waiting for transfers between devices: 29.2 us -> 17 us  [local(): w_perm = lax.all_gather(w_mine, 'row', axis=1, tiled=True)]
    reduce_scatter x1, waiting for transfers between devices: 9.42 us -> 1.18 us  [local(): out_sum = lax.psum_scatter(out_part, 'col', scatter_dimension=0, tiled=True)]
    ppermute x1, waiting for transfers between devices: 0.01 us -> 7.23 us  [local(): lax.ppermute(jnp.where(even, g_gate, g_src), 'row', reverse_moves(moves_t...]
  transfers between devices with their start and end apart: 23 -> 21, of which waited for: 13 -> 13; matrix products, arithmetic and copies ran while one was open for 7% -> 11% of each run, Pallas kernels for 25% -> 27%
where the time goes in v1:
time: 392 us; the launch traced here: 389 us
  Pallas kernels  105 us (27%)
  waiting for transfers between devices  102 us (26%)
  blocking collectives  59.4 us (15%)
  starting transfers between devices  45.8 us (12%)
  other arithmetic  31.4 us (8%)
  local copies, waits for them, and re-layouts  20.6 us (5%)
  between operations  14.9 us (4%)
  matrix products  10.1 us (3%)
    pallas_call x2, Pallas kernels, run_backward(): pl.pallas_call(lambda *refs: backward_kernel(states, *refs), grid=(2,), i...  69.7 us
    pallas_call x2, Pallas kernels, run_forward(): pl.pallas_call(lambda *refs: forward_kernel(states, *refs), grid=(2,), in...  35.2 us
    psum x1, waiting for transfers between devices, local(): in_sum = lax.psum(in_part, 'col')  20.8 us
    all_gather x1, waiting for transfers between devices, local(): w_perm = lax.all_gather(w_mine, 'row', axis=1, tiled=True)  17 us
    all_gather x1, waiting for transfers between devices, local(): field_all = lax.all_gather(field, 'row', axis=0, tiled=True)  16.9 us
    all_to_all x1, waiting for transfers between devices, local(): lax.all_to_all(jnp.concatenate([active, proj[..., split:]], axis=-1), 'co...  14.4 us
    all_to_all x1, blocking collectives, local(): lax.all_to_all(dproj.astype(BF16).reshape(nr, rows, cols, dirs * coefs),...  12.3 us
    all_gather x1, blocking collectives, local(): out_rows = lax.all_gather(out_sum.astype(BF16), 'row', axis=0)  10.6 us
  transfers between devices with their start and end apart: 21, of which 13 were waited for; matrix products, arithmetic and copies ran while one was open for 11% of the time, Pallas kernels for 27%

profile of v1, /device:TPU:0, one launch (start us, length us, event | category | flops | bytes accessed | tf_op | source)
XLA Modules:
  0.0 389.0 jit_solution(4231043237653622320)
XLA Ops:
  10.7 4.4 %collective-permute-start.1 = (bf16[512,128]{0,1:T(8,128)(2,1)S(1)}, bf16[512,128]{0,1:T(8,128)(2,1)S(1)}, u32[]{:S(2)}, u32[]{:S(2)}) collective-permute-start(bf16[512,128]{0,1:T(8,128)(2,1)S(1)} %get-tuple-element.87), channel_id=1, source_target_pairs={{0,4},{4,12},{8,20},{12,28},{16,0},{20,8},{24,16},{28,24},{1,5},{5... | collective-permute-start | bytes 393224 | tf_op jit(solution)/shard_map/ppermute | solution.py:340
  19.2 16.9 %all-gather.7.cloned.1.call-done = bf16[64,16,512]{2,1,0:T(8,128)(2,1)} async-done(((bf16[8,16,512]{2,1,0:T(8,128)(2,1)}), bf16[64,16,512]{2,1,0:T(8,128)(2,1)}) %all-gather.7.cloned.1.call-update) | async-done | bytes 1048592 | tf_op jit(solution)/shard_map/all_gather | solution.py:337
  43.1 4.1 %collective-permute-done.2 = bf16[64,1,128]{2,1,0:T(2,128)(2,1)S(1)} collective-permute-done((bf16[64,1,128]{2,1,0:T(2,128)(2,1)S(1)}, bf16[64,1,128]{2,1,0:T(2,128)(2,1)S(1)}, u32[]{:S(2)}, u32[]{:S(2)}) %collective-permute-start.2) | collective-permute-done | bytes 16416 | tf_op jit(solution)/shard_map/ppermute | solution.py:314
  55.7 3.9 %all-to-all-done = bf16[64,16,128]{2,1,0:T(8,128)(2,1)S(1)} async-done(((bf16[64,16,128]{2,1,0:T(8,128)(2,1)}), bf16[64,16,128]{2,1,0:T(8,128)(2,1)S(1)}, u32[]{:S(2)}, u32[]{:S(2)}) %all-to-all-start) | async-done | bytes 262176 | tf_op jit(solution)/shard_map/all_to_all | solution.py:359
  60.0 8.9 %all_gather.31 = bf16[64,16,256]{2,1,0:T(8,128)(2,1)S(1)} all-gather(bf16[8,16,256]{2,1,0:T(8,128)(2,1)S(1)} %bitcast.185), channel_id=1, replica_groups=mesh['row'=8,'col'=4] {'row'}, dimensions={0}, use_global_device_ids=true | all-gather | bytes 589824 | tf_op jit(solution)/shard_map/all_gather | solution.py:361
  75.2 14.4 %all-to-all-done.1 = bf16[64,16,256]{2,1,0:T(8,128)(2,1)S(1)} async-done(((bf16[64,16,256]{2,1,0:T(8,128)(2,1)}), bf16[64,16,256]{2,1,0:T(8,128)(2,1)S(1)}, u32[]{:S(2)}, u32[]{:S(2)}) %all-to-all-start.1) | async-done | bytes 524320 | tf_op jit(solution)/shard_map/all_to_all | solution.py:365
  93.5 17.6 %scan_forward.3 = (f32[64,16,128]{2,1,0:T(8,128)}, f32[2,16,16,128]{3,2,1,0:T(8,128)}) custom-call(bf16[64,16,128]{2,1,0:T(8,128)(2,1)} %slice.323.refs_0_, bf16[2,64,16,64]{3,2,1,0:T(8,128)(2,1)} %pad_maximum_fusion.8.refs_1_, bf16[2,64,128]{2,1,0:T(8,128)(2,1)} %copy.95.refs_2_, f32[2,8,128]{2,1,0:T(8,128)} %broadcast_in_dim.55.refs_3_.refs_4_, ...), custom_call_target="tpu_custom_call" | custom-call | flops 83886080 | bytes 2097152 | tf_op jit(solution)/shard_map/scan_forward/pallas_call | solution.py:219
  121.3 17.6 %scan_forward.2 = (f32[64,16,128]{2,1,0:T(8,128)}, f32[2,16,16,128]{3,2,1,0:T(8,128)}) custom-call(bf16[64,16,128]{2,1,0:T(8,128)(2,1)} %get-tuple-element.59.refs_0_, bf16[2,64,16,64]{3,2,1,0:T(8,128)(2,1)} %pad_maximum_fusion.6.refs_1_, bf16[2,64,128]{2,1,0:T(8,128)(2,1)} %copy.93.refs_2_, f32[2,8,128]{2,1,0:T(8,128)} %broadcast_in_dim.24.refs_3_.refs_4_, ...), custom_call_target="tpu_custom_call" | custom-call | flops 83886080 | bytes 2097152 | tf_op jit(solution)/shard_map/scan_forward/pallas_call | solution.py:219
  141.2 9.3 %all-gather = f32[32,64,16]{1,2,0:T(8,128)S(1)} all-gather(f32[4,64,16]{1,2,0:T(8,128)S(1)} %pad_maximum_fusion.19), channel_id=2, replica_groups=mesh['row'=8,'col'=4] {'row'}, dimensions={0}, use_global_device_ids=true | all-gather | bytes 147456 | tf_op jit(solution)/shard_map/all_gather | solution.py:411
  161.6 9.5 %all_to_all.128 = bf16[64,16,128]{2,1,0:T(8,128)(2,1)S(1)} all-to-all(bf16[64,16,128]{2,1,0:T(8,128)(2,1)S(1)} %get-tuple-element.63), channel_id=1, replica_groups=mesh['row'=8,'col'=4] {'row'}, dimensions={0} | all-to-all | bytes 524288 | tf_op jit(solution)/shard_map/all_to_all | solution.py:431
  171.1 5.0 %all-to-all-start.5 = ((bf16[64,16,128]{2,1,0:T(8,128)(2,1)}), bf16[64,16,128]{2,1,0:T(8,128)(2,1)S(1)}, u32[]{:S(2)}, u32[]{:S(2)}) async-start(bf16[64,16,128]{2,1,0:T(8,128)(2,1)} %get-tuple-element.22.refs_8_), calls=%async_computation.6 | async-start | bytes 524288 | tf_op jit(solution)/shard_map/all_to_all | solution.py:425
  181.0 10.6 %all-gather.1 = bf16[256,512]{1,0:T(8,128)(2,1)} all-gather(bf16[32,512]{1,0:T(8,128)(2,1)S(1)} %convert_element_type.131), channel_id=3, replica_groups=mesh['row'=8,'col'=4] {'row'}, dimensions={0}, use_global_device_ids=true | all-gather | bytes 294912 | tf_op jit(solution)/shard_map/all_gather | solution.py:436
  191.6 17.0 %all-gather.13.cloned.1.call-done = bf16[512,2048]{0,1:T(8,128)(2,1)} async-done(((bf16[512,256]{0,1:T(8,128)(2,1)}), bf16[512,2048]{0,1:T(8,128)(2,1)}) %all-gather.13.cloned.1.call-update) | async-done | bytes 2097168 | tf_op jit(solution)/shard_map/all_gather | solution.py:349
  208.6 4.6 %all-to-all-start.4 = ((bf16[8,32,512]{2,1,0:T(8,128)(2,1)}), bf16[8,32,512]{2,1,0:T(8,128)(2,1)S(1)}, u32[]{:S(2)}, u32[]{:S(2)}) async-start(bf16[8,32,512]{2,1,0:T(8,128)(2,1)} %bitcast.42), calls=%async_computation.5 | async-start | bytes 524288 | tf_op jit(solution)/shard_map/all_to_all | solution.py:438
  214.6 34.9 %scan_backward.3 = (f32[64,16,128]{2,1,0:T(8,128)}, f32[2,64,16,64]{3,2,1,0:T(8,128)}) custom-call(bf16[64,16,128]{2,1,0:T(8,128)(2,1)} %slice.323.refs_0_, bf16[2,64,16,64]{3,2,1,0:T(8,128)(2,1)} %pad_maximum_fusion.8.refs_1_, bf16[2,64,128]{2,1,0:T(8,128)(2,1)} %copy.95.refs_2_, bf16[2,128,64]{2,1,0:T(8,128)(2,1)} %get-tuple-element.90.refs_3_, ...), custom_call_target="tpu_custom_call" | custom-call | flops 125829120 | bytes 4194304 | tf_op jit(solution)/shard_map/scan_backward/pallas_call | solution.py:251
  252.9 5.1 %all-to-all-start.6 = ((bf16[16,64,256]{2,0,1:T(8,128)(2,1)}), bf16[16,64,256]{2,0,1:T(8,128)(2,1)S(1)}, u32[]{:S(2)}, u32[]{:S(2)}) async-start(bf16[16,64,256]{2,0,1:T(8,128)(2,1)} %maximum_bitcast_fusion), calls=%async_computation.7 | async-start | bytes 1048576 | tf_op jit(solution)/shard_map/all_to_all | solution.py:444
  258.0 34.9 %scan_backward.2 = (f32[64,16,128]{2,1,0:T(8,128)}, f32[2,64,16,64]{3,2,1,0:T(8,128)}) custom-call(bf16[64,16,128]{2,1,0:T(8,128)(2,1)} %get-tuple-element.59.refs_0_, bf16[2,64,16,64]{3,2,1,0:T(8,128)(2,1)} %pad_maximum_fusion.6.refs_1_, bf16[2,64,128]{2,1,0:T(8,128)(2,1)} %copy.93.refs_2_, bf16[2,128,64]{2,1,0:T(8,128)(2,1)} %get-tuple-element.91.refs_3_, ...), custom_call_target="tpu_custom_call" | custom-call | flops 125829120 | bytes 4194304 | tf_op jit(solution)/shard_map/scan_backward/pallas_call | solution.py:251
  294.7 12.3 %all_to_all.129 = bf16[8,8,16,256]{3,2,1,0:T(8,128)(2,1)S(1)} all-to-all(bf16[8,8,16,256]{3,2,1,0:T(8,128)(2,1)S(1)} %pad_maximum_fusion.9), channel_id=1, replica_groups=mesh['row'=8,'col'=4] {'row'}, dimensions={0} | all-to-all | bytes 1048576 | tf_op jit(solution)/shard_map/all_to_all | solution.py:449
  307.0 8.9 %all_gather.39 = bf16[64,16,256]{2,1,0:T(8,128)(2,1)S(1)} all-gather(bf16[8,16,256]{2,1,0:T(8,128)(2,1)S(1)} %reduce_sum.102), channel_id=1, replica_groups=mesh['row'=8,'col'=4] {'row'}, dimensions={0}, use_global_device_ids=true | all-gather | bytes 589824 | tf_op jit(solution)/shard_map/all_gather | solution.py:453
  323.1 4.1 %collective-permute-done.4 = f32[64,1,128]{2,1,0:T(1,128)S(1)} collective-permute-done((f32[64,1,128]{2,1,0:T(1,128)S(1)}, f32[64,1,128]{2,1,0:T(1,128)S(1)}, u32[]{:S(2)}, u32[]{:S(2)}) %collective-permute-start.4) | collective-permute-done | bytes 32800 | tf_op jit(solution)/shard_map/ppermute | solution.py:314
  337.2 6.7 %all-to-all-done.8 = bf16[64,16,256]{2,1,0:T(8,128)(2,1)S(1)} async-done(((bf16[64,16,256]{2,1,0:T(8,128)(2,1)}), bf16[64,16,256]{2,1,0:T(8,128)(2,1)S(1)}, u32[]{:S(2)}, u32[]{:S(2)}) %all-to-all-start.8) | async-done | bytes 524320 | tf_op jit(solution)/shard_map/all_to_all | solution.py:469
  344.8 20.8 %all-reduce.3.cloned.1.call-done = f32[512,256]{0,1:T(8,128)} async-done(((f32[512,256]{0,1:T(8,128)}), f32[512,256]{0,1:T(8,128)}) %all-reduce.3.cloned.1.call-update) | async-done | bytes 524304 | tf_op jit(solution)/shard_map/psum | solution.py:476
  367.4 4.2 %collective-permute-start.7 = (f32[512,128]{0,1:T(8,128)S(1)}, f32[512,128]{0,1:T(8,128)S(1)}, u32[]{:S(2)}, u32[]{:S(2)}) collective-permute-start(f32[512,128]{0,1:T(8,128)S(1)} %get-tuple-element.69), channel_id=1, source_target_pairs={{4,0},{12,4},{20,8},{28,12},{0,16},{8,20},{16,24},{24,28},{5,1},{1... | collective-permute-start | bytes 786440 | tf_op jit(solution)/shard_map/ppermute | solution.py:479
  373.8 7.2 %collective-permute-done.7 = f32[512,128]{0,1:T(8,128)S(1)} collective-permute-done((f32[512,128]{0,1:T(8,128)S(1)}, f32[512,128]{0,1:T(8,128)S(1)}, u32[]{:S(2)}, u32[]{:S(2)}) %collective-permute-start.7) | collective-permute-done | bytes 262176 | tf_op jit(solution)/shard_map/ppermute | solution.py:479
  (192 shorter events, 91.3 us)
Async XLA Ops:
  7.2 52.6 %copy-start = (bf16[1024,256]{1,0:T(8,128)(2,1)S(1)}, bf16[1024,256]{1,0:T(8,128)(2,1)}, u32[]{:S(2)}) copy-start(bf16[1024,256]{1,0:T(8,128)(2,1)} %param.14) | copy-start | bytes 1572868
  7.2 28.9 %all-gather.7.cloned.1.call-start = ((), (), s32[]{:S(2)}) async-start(), calls=%async_computation.10 | async-start | bytes 1179648 | tf_op jit(solution)/shard_map/all_gather | solution.py:337
  7.9 108.4 %all-gather.9.cloned.1.call-start = ((), (), s32[]{:S(2)}) async-start(), calls=%async_computation.11 | async-start | bytes 1310720 | tf_op jit(solution)/shard_map/all_gather | solution.py:348
  8.7 107.7 %all-gather.11.cloned.1.call-start = ((), (), s32[]{:S(2)}) async-start(), calls=%async_computation.12 | async-start | bytes 1179648 | tf_op jit(solution)/shard_map/all_gather | solution.py:347
  10.0 6.8 %collective-permute-start = (bf16[512,128]{0,1:T(8,128)(2,1)S(1)}, bf16[512,128]{0,1:T(8,128)(2,1)S(1)}, u32[]{:S(2)}, u32[]{:S(2)}) collective-permute-start(bf16[512,128]{0,1:T(8,128)(2,1)S(1)} %get-tuple-element.86), channel_id=1, source_target_pairs={{0,0},{4,8},{8,16},{12,24},{16,4},{20,12},{24,20},{28,28},{1,1},{5... | collective-permute-start | bytes 393224 | tf_op jit(solution)/shard_map/ppermute | solution.py:339
  10.7 8.5 %collective-permute-start.1 = (bf16[512,128]{0,1:T(8,128)(2,1)S(1)}, bf16[512,128]{0,1:T(8,128)(2,1)S(1)}, u32[]{:S(2)}, u32[]{:S(2)}) collective-permute-start(bf16[512,128]{0,1:T(8,128)(2,1)S(1)} %get-tuple-element.87), channel_id=1, source_target_pairs={{0,4},{4,12},{8,20},{12,28},{16,0},{20,8},{24,16},{28,24},{1,5},{5... | collective-permute-start | bytes 393224 | tf_op jit(solution)/shard_map/ppermute | solution.py:340
  38.1 5.0 %collective-permute-start.3 = (bf16[64,1,128]{2,1,0:T(2,128)(2,1)S(1)}, bf16[64,1,128]{2,1,0:T(2,128)(2,1)S(1)}, u32[]{:S(2)}, u32[]{:S(2)}) collective-permute-start(bf16[64,1,128]{2,1,0:T(2,128)(2,1)S(1)} %get-tuple-element.81), channel_id=1, source_target_pairs={{1,0},{2,1},{3,2},{0,3},{5,4},{6,5},{7,6},{4,7},{9,8},{10,9},{11,1... | collective-permute-start | bytes 49160 | tf_op jit(solution)/shard_map/ppermute | solution.py:315
  41.5 5.7 %collective-permute-start.2 = (bf16[64,1,128]{2,1,0:T(2,128)(2,1)S(1)}, bf16[64,1,128]{2,1,0:T(2,128)(2,1)S(1)}, u32[]{:S(2)}, u32[]{:S(2)}) collective-permute-start(bf16[64,1,128]{2,1,0:T(2,128)(2,1)S(1)} %get-tuple-element.80), channel_id=1, source_target_pairs={{0,1},{1,2},{2,3},{3,0},{4,5},{5,6},{6,7},{7,4},{8,9},{9,10},{10,1... | collective-permute-start | bytes 49160 | tf_op jit(solution)/shard_map/ppermute | solution.py:314
  49.3 10.3 %all-to-all-start = ((bf16[64,16,128]{2,1,0:T(8,128)(2,1)}), bf16[64,16,128]{2,1,0:T(8,128)(2,1)S(1)}, u32[]{:S(2)}, u32[]{:S(2)}) async-start(bf16[64,16,128]{2,1,0:T(8,128)(2,1)} %get-tuple-element.59.refs_0_), calls=%async_computation | async-start | bytes 524288 | tf_op jit(solution)/shard_map/all_to_all | solution.py:359
  55.7 84.6 %copy-start.28 = (f32[128]{0:T(128)}, f32[128]{0:T(128)S(1)}, u32[]{:S(2)}) copy-start(f32[128]{0:T(128)S(1)} %dynamic_slice.30) | copy-start | bytes 1540
  70.8 18.7 %all-to-all-start.1 = ((bf16[64,16,256]{2,1,0:T(8,128)(2,1)}), bf16[64,16,256]{2,1,0:T(8,128)(2,1)S(1)}, u32[]{:S(2)}, u32[]{:S(2)}) async-start(bf16[64,16,256]{2,1,0:T(8,128)(2,1)} %pad_maximum_fusion.7), calls=%async_computation.1 | async-start | bytes 1048576 | tf_op jit(solution)/shard_map/all_to_all | solution.py:365
  112.8 26.1 %all-to-all-start.2 = ((bf16[16,64,128]{2,0,1:T(8,128)(2,1)}), bf16[16,64,128]{2,0,1:T(8,128)(2,1)S(1)}, u32[]{:S(2)}, u32[]{:S(2)}) async-start(bf16[16,64,128]{2,0,1:T(8,128)(2,1)} %convert_bitcast_fusion), calls=%async_computation.2 | async-start | bytes 524288 | tf_op jit(solution)/shard_map/all_to_all | solution.py:393
  116.3 63.9 %reduce-scatter.2.cloned.1.call-start = ((), (), s32[]{:S(2)}) async-start(), calls=%async_computation.13 | async-start | bytes 327680 | tf_op jit(solution)/shard_map/reduce_scatter | solution.py:435
  159.9 48.7 %all-gather.13.cloned.1.call-start = ((), (), s32[]{:S(2)}) async-start(), calls=%async_computation.14 | async-start | bytes 2359296 | tf_op jit(solution)/shard_map/all_gather | solution.py:349
  171.1 37.5 %all-to-all-start.5 = ((bf16[64,16,128]{2,1,0:T(8,128)(2,1)}), bf16[64,16,128]{2,1,0:T(8,128)(2,1)S(1)}, u32[]{:S(2)}, u32[]{:S(2)}) async-start(bf16[64,16,128]{2,1,0:T(8,128)(2,1)} %get-tuple-element.22.refs_8_), calls=%async_computation.6 | async-start | bytes 524288 | tf_op jit(solution)/shard_map/all_to_all | solution.py:425
  208.6 44.3 %all-to-all-start.4 = ((bf16[8,32,512]{2,1,0:T(8,128)(2,1)}), bf16[8,32,512]{2,1,0:T(8,128)(2,1)S(1)}, u32[]{:S(2)}, u32[]{:S(2)}) async-start(bf16[8,32,512]{2,1,0:T(8,128)(2,1)} %bitcast.42), calls=%async_computation.5 | async-start | bytes 524288 | tf_op jit(solution)/shard_map/all_to_all | solution.py:438
  252.9 41.3 %all-to-all-start.6 = ((bf16[16,64,256]{2,0,1:T(8,128)(2,1)}), bf16[16,64,256]{2,0,1:T(8,128)(2,1)S(1)}, u32[]{:S(2)}, u32[]{:S(2)}) async-start(bf16[16,64,256]{2,0,1:T(8,128)(2,1)} %maximum_bitcast_fusion), calls=%async_computation.7 | async-start | bytes 1048576 | tf_op jit(solution)/shard_map/all_to_all | solution.py:444
  258.0 107.6 %all-reduce.3.cloned.1.call-start = ((), (), s32[]{:S(2)}) async-start(), calls=%async_computation.15 | async-start | bytes 1048576 | tf_op jit(solution)/shard_map/psum | solution.py:476
  317.6 5.5 %collective-permute-start.5 = (f32[64,1,128]{2,1,0:T(1,128)S(1)}, f32[64,1,128]{2,1,0:T(1,128)S(1)}, u32[]{:S(2)}, u32[]{:S(2)}) collective-permute-start(f32[64,1,128]{2,1,0:T(1,128)S(1)} %get-tuple-element.71), channel_id=1, source_target_pairs={{1,0},{2,1},{3,2},{0,3},{5,4},{6,5},{7,6},{4,7},{9,8},{10,9},{11,1... | collective-permute-start | bytes 98312 | tf_op jit(solution)/shard_map/ppermute | solution.py:315
  321.5 5.7 %collective-permute-start.4 = (f32[64,1,128]{2,1,0:T(1,128)S(1)}, f32[64,1,128]{2,1,0:T(1,128)S(1)}, u32[]{:S(2)}, u32[]{:S(2)}) collective-permute-start(f32[64,1,128]{2,1,0:T(1,128)S(1)} %get-tuple-element.70), channel_id=1, source_target_pairs={{0,1},{1,2},{2,3},{3,0},{4,5},{5,6},{6,7},{7,4},{8,9},{9,10},{10,1... | collective-permute-start | bytes 98312 | tf_op jit(solution)/shard_map/ppermute | solution.py:314
  330.8 13.2 %all-to-all-start.8 = ((bf16[64,16,256]{2,1,0:T(8,128)(2,1)}), bf16[64,16,256]{2,1,0:T(8,128)(2,1)S(1)}, u32[]{:S(2)}, u32[]{:S(2)}) async-start(bf16[64,16,256]{2,1,0:T(8,128)(2,1)} %pad_maximum_fusion.10), calls=%async_computation.9 | async-start | bytes 1048576 | tf_op jit(solution)/shard_map/all_to_all | solution.py:469
  334.6 37.0 %copy-start.2 = (bf16[512,2048]{0,1:T(8,128)(2,1)S(1)}, bf16[512,2048]{0,1:T(8,128)(2,1)}, u32[]{:S(2)}) copy-start(bf16[512,2048]{0,1:T(8,128)(2,1)} %all-gather.13.cloned.1.call-done) | copy-start | bytes 6291460
  366.7 7.1 %collective-permute-start.6 = (f32[512,128]{0,1:T(8,128)S(1)}, f32[512,128]{0,1:T(8,128)S(1)}, u32[]{:S(2)}, u32[]{:S(2)}) collective-permute-start(f32[512,128]{0,1:T(8,128)S(1)} %get-tuple-element.68), channel_id=1, source_target_pairs={{0,0},{8,4},{16,8},{24,12},{4,16},{12,20},{20,24},{28,28},{1,1},{9... | collective-permute-start | bytes 786440 | tf_op jit(solution)/shard_map/ppermute | solution.py:478
  367.4 13.7 %collective-permute-start.7 = (f32[512,128]{0,1:T(8,128)S(1)}, f32[512,128]{0,1:T(8,128)S(1)}, u32[]{:S(2)}, u32[]{:S(2)}) collective-permute-start(f32[512,128]{0,1:T(8,128)S(1)} %get-tuple-element.69), channel_id=1, source_target_pairs={{4,0},{12,4},{20,8},{28,12},{0,16},{8,20},{16,24},{24,28},{5,1},{1... | collective-permute-start | bytes 786440 | tf_op jit(solution)/shard_map/ppermute | solution.py:479
  (26 other events, 250.6 us)
Sparse Core Ops, SparseCore 0:
  9.9 26.1 all-gather.6
  37.7 27.9 all-gather.8
  67.5 22.9 all-gather.10
  160.0 20.1 reduce-scatter.1
  182.0 26.4 all-gather.12
  330.1 35.4 all-reduce.2

commit v2 on v1

--- a/solution.py
+++ b/solution.py
@@ -296,24 +296,115 @@
     return jnp.swapaxes(values, 0, 1)
 
 
-def weight_moves(peers):
-    half = peers // 2
-    one = [(r, 2 * r if r < half else 2 * (r - half) + 1) for r in range(peers)]
-    two = [(r, 2 * r + 1 if r < half else 2 * (r - half)) for r in range(peers)]
-    return one, two
-
-
-def reverse_moves(moves):
-    return [(b, a) for a, b in moves]
-
-
-def col_halo(cells):
-    peers = lax.axis_size("col")
-    up = [(i, (i + 1) % peers) for i in range(peers)]
-    down = [((i + 1) % peers, i) for i in range(peers)]
-    before = lax.ppermute(cells[:, -1:], "col", up)
-    after = lax.ppermute(cells[:, :1], "col", down)
-    wide = jnp.concatenate([before, cells, after], axis=1)
+def exchange_kernel(plan, sizes, *refs):
+    count = len(plan)
+    ins, outs = refs[:count], refs[count : 2 * count]
+    send, recv, own = refs[2 * count :]
+    axes = sorted({axis for _, axis in plan})
+    mesh_ids = pl.DeviceIdType.MESH
+    place = {axis: lax.axis_index(axis) for axis in axes}
+    barrier = pltpu.get_barrier_semaphore()
+    greeted = 0
+    for axis in axes:
+        for off in range(1, sizes[axis]):
+            peer = lax.rem(place[axis] + off, sizes[axis])
+            pl.semaphore_signal(barrier, inc=1, device_id={axis: peer}, device_id_type=mesh_ids)
+            greeted += 1
+    pl.semaphore_wait(barrier, greeted)
+
+    copies, locals_, guarded = [], [], []
+    for i, (kind, axis) in enumerate(plan):
+        me, peers = place[axis], sizes[axis]
+        half = peers // 2
+
+        def remote(src, dst, sent, got, peer, i=i, axis=axis):
+            return pltpu.make_async_remote_copy(
+                src_ref=src, dst_ref=dst, send_sem=send.at[i, sent], recv_sem=recv.at[i, got],
+                device_id={axis: peer}, device_id_type=mesh_ids,
+            )
+
+        if kind in ("spread", "gather"):
+            for off in range(1, peers):
+                peer = lax.rem(me + off, peers)
+                src = ins[i].at[peer] if kind == "spread" else ins[i]
+                copies.append(remote(src, outs[i].at[me], off, off, peer))
+            src = ins[i].at[me] if kind == "spread" else ins[i]
+            locals_.append(pltpu.make_async_copy(src, outs[i].at[me], own.at[i]))
+        elif kind == "halo":
+            copies.append(remote(ins[i].at[1], outs[i].at[0], 0, 0, lax.rem(me + 1, peers)))
+            copies.append(remote(ins[i].at[0], outs[i].at[1], 1, 1, lax.rem(me + peers - 1, peers)))
+        else:
+            for b in range(2):
+                if kind == "deal":
+                    to, slot, origin = lax.rem(2 * me + b, peers), me // half, b * half + me // 2
+                else:
+                    to, slot, origin = b * half + me // 2, lax.rem(me, 2), lax.rem(2 * me + b, peers)
+                out = remote(ins[i].at[b], outs[i].at[slot], b, slot, to)
+                here = pltpu.make_async_copy(ins[i].at[b], outs[i].at[slot], own.at[i])
+                arrive = remote(ins[i].at[b], outs[i].at[b], b, b, to)
+                guarded.append((to, me, out, here, origin, arrive))
+    for copy in copies:
+        copy.start()
+    for to, me, out, here, _, _ in guarded:
+        pl.when(to != me)(out.start)
+        pl.when(to == me)(here.start)
+    for copy in locals_:
+        copy.start()
+    for copy in copies:
+        copy.wait()
+    for to, me, out, here, origin, arrive in guarded:
+        pl.when(to != me)(out.wait_send)
+        pl.when(to == me)(here.wait)
+        pl.when(origin != me)(arrive.wait_recv)
+    for copy in locals_:
+        copy.wait()
+
+
+def exchange(stage, *items):
+    plan = tuple((kind, axis) for kind, axis, _ in items)
+    arrays = [values for _, _, values in items]
+    sizes = {axis: lax.axis_size(axis) for _, axis in plan}
+    shapes = [
+        jax.ShapeDtypeStruct(
+            (sizes[axis],) + values.shape if kind == "gather" else values.shape, values.dtype
+        )
+        for kind, axis, values in items
+    ]
+    most = max(max(sizes.values()), 2)
+    anywhere = pl.BlockSpec(memory_space=pl.ANY)
+    return pl.pallas_call(
+        lambda *refs: exchange_kernel(plan, sizes, *refs),
+        in_specs=[anywhere] * len(items),
+        out_specs=[anywhere] * len(items),
+        out_shape=shapes,
+        scratch_shapes=[
+            pltpu.SemaphoreType.DMA((len(items), most)),
+            pltpu.SemaphoreType.DMA((len(items), most)),
+            pltpu.SemaphoreType.DMA((len(items),)),
+        ],
+        compiler_params=pltpu.CompilerParams(collective_id=stage, has_side_effects=True),
+        name="exchange_%d" % stage,
+    )(*arrays)
+
+
+def parts(values, axis, count):
+    shape = values.shape
+    cut = values.reshape(shape[:axis] + (count, shape[axis] // count) + shape[axis + 1 :])
+    return jnp.moveaxis(cut, axis, 0)
+
+
+def joined(values, axis):
+    moved = jnp.moveaxis(values, 0, axis)
+    shape = moved.shape
+    return moved.reshape(shape[:axis] + (shape[axis] * shape[axis + 1],) + shape[axis + 2 :])
+
+
+def edges(cells):
+    return jnp.stack([cells[:, 0], cells[:, -1]])
+
+
+def with_edges(cells, got):
+    wide = jnp.concatenate([got[0][:, None], cells, got[1][:, None]], axis=1)
     return jnp.concatenate([wide[-1:], wide, wide[:1]], axis=0)
 
 
@@ -327,20 +418,15 @@
     nr, nc = lax.axis_size("row"), lax.axis_size("col")
     me = lax.axis_index("row")
     all_rows, width = rows * nr, e_dim // nr
-    even = me % 2 == 0
-    low = me < nr // 2
-    moves_one, moves_two = weight_moves(nr)
 
     def mine(values):
         return lax.dynamic_slice_in_dim(values, me * width, width, axis=values.ndim - 1)
 
-    field_all = lax.all_gather(field, "row", axis=0, tiled=True)
-    left, right = in_weight[:, :width], in_weight[:, width:]
-    got_one = lax.ppermute(jnp.where(low, left, right), "row", moves_one)
-    got_two = lax.ppermute(jnp.where(low, right, left), "row", moves_two)
-    w_mine = jnp.concatenate(
-        [jnp.where(even, got_one, got_two), jnp.where(even, got_two, got_one)], axis=1
-    )
+    dealt, field_all = exchange(
+        0, ("deal", "row", parts(in_weight, 1, 2)), ("gather", "row", field)
+    )
+    field_all = field_all.reshape(all_rows, cols, c_dim)
+    w_mine = jnp.concatenate([dealt[0], dealt[1]], axis=1)
     field_flat = field_all.reshape(-1, c_dim)
     xz = jnp.dot(field_flat, w_mine, preferred_element_type=F32).astype(BF16).reshape(all_rows, cols, 2 * width)
     source, gate = xz[..., :width], xz[..., width:].astype(F32)
@@ -349,26 +435,27 @@
     w_perm = lax.all_gather(w_mine, "row", axis=1, tiled=True)
 
     taps = mine(conv_weight)
-    padded = col_halo(source)
+    (source_edges,) = exchange(1, ("halo", "col", edges(source)))
+    padded = with_edges(source, source_edges)
     convolved = jnp.zeros(source.shape, F32)
     for a in range(3):
         for b in range(3):
             convolved = convolved + padded[a : a + all_rows, b : b + cols].astype(F32) * taps[a, b]
     active = jax.nn.silu(convolved).astype(BF16)
 
-    act_cells = lax.all_to_all(active, "row", 0, 2, tiled=True)
+    act_row, act_col = exchange(
+        2, ("spread", "row", parts(active, 0, nr)), ("spread", "col", parts(active, 0, nc))
+    )
+    act_cells = joined(act_row, 2)
     proj_cells = jnp.dot(act_cells.reshape(-1, e_dim), proj_weight, preferred_element_type=F32)
-    proj = lax.all_gather(
-        proj_cells.astype(BF16).reshape(rows, cols, dirs * coefs), "row", axis=0, tiled=True
-    )
     split = 2 * coefs
-    across = lax.all_to_all(
-        jnp.concatenate([active, proj[..., split:]], axis=-1), "col", 0, 1, tiled=True
-    )
-    across = swap(across)
-    act_down, act_across = active, across[..., :width]
+    (proj,) = exchange(3, ("gather", "row", proj_cells.astype(BF16).reshape(rows, cols, 2 * split)))
+    proj = proj.reshape(all_rows, cols, 2 * split)
+    (proj_col,) = exchange(4, ("spread", "col", parts(proj[..., split:], 0, nc)))
+    act_down = active
+    act_across, across = swap(joined(act_col, 1)), swap(joined(proj_col, 1))
     pair = lambda values: jnp.stack([values[..., :coefs], values[..., coefs:]], axis=0)
-    proj_down, proj_across = pair(proj[..., :split]), pair(across[..., width:])
+    proj_down, proj_across = pair(proj[..., :split]), pair(across)
 
     lanes = -(-width // LANES) * LANES
     lines = cols
@@ -390,8 +477,8 @@
     spread = pick.T
     y_across, start_across = run_forward(act_across, proj_across, params_across, spread)
     y_down, start_down = run_forward(act_down, proj_down, params_down, spread)
-    y_back = lax.all_to_all(swap(y_across[..., :width].astype(BF16)), "col", 1, 0, tiled=True)
-    summed = y_down[..., :width] + y_back.astype(F32)
+    (y_back,) = exchange(5, ("spread", "col", parts(swap(y_across[..., :width].astype(BF16)), 1, nc)))
+    summed = y_down[..., :width] + joined(y_back, 0).astype(F32)
 
     back_mixed = lax.dot_general(
         grad_all.reshape(-1, c_dim),
@@ -408,7 +495,8 @@
     stats = jnp.stack(
         [own_mean, jnp.sum(shifted * shifted, -1), jnp.sum(back_norm, -1), jnp.sum(back_norm * shifted, -1)]
     )
-    stats = lax.all_gather(stats, "row", axis=0)
+    (stats,) = exchange(6, ("gather", "row", stats.reshape(-1, LANES)))
+    stats = stats.reshape(nr, 4, all_rows, cols)
     means = stats[:, 0]
     centre = jnp.mean(means, axis=0)
     off = means - centre
@@ -422,35 +510,40 @@
     back_gate = back_mixed * normed * (sig * (1.0 + gate * (1.0 - sig)))
     back_summed = scale[..., None] * (back_norm - flat_mean[..., None] - hat * tilt_mean[..., None])
     back_bf = back_summed.astype(BF16)
-    gy_across = swap(lax.all_to_all(back_bf, "col", 0, 1, tiled=True))
+    contract = (((0,), (0,)), ((), ()))
+    out_part = lax.dot_general(
+        mixed.reshape(-1, width), grad_all.reshape(-1, c_dim), contract, preferred_element_type=F32
+    )
+    gy_across, mixed_cells, out_parts = exchange(
+        7,
+        ("spread", "col", parts(back_bf, 0, nc)),
+        ("spread", "row", parts(mixed, 0, nr)),
+        ("spread", "col", parts(out_part.astype(BF16), 0, nc)),
+    )
+    gy_across = swap(joined(gy_across, 1))
+    mixed_cells = joined(mixed_cells, 2).reshape(-1, e_dim)
+    out_sum = jnp.sum(out_parts.astype(F32), axis=0).astype(BF16)
 
     dact_across, dproj_across = run_backward(
         act_across, proj_across, params_across, start_across, pad_to(gy_across, 2, lanes), pick, spread
     )
-    contract = (((0,), (0,)), ((), ()))
-    mixed_cells = lax.all_to_all(mixed, "row", 0, 2, tiled=True).reshape(-1, e_dim)
-    out_part = lax.dot_general(
-        mixed.reshape(-1, width), grad_all.reshape(-1, c_dim), contract, preferred_element_type=F32
-    )
-    out_sum = lax.psum_scatter(out_part, "col", scatter_dimension=0, tiled=True)
-    out_rows = lax.all_gather(out_sum.astype(BF16), "row", axis=0)
-    back_bf, out_rows, mixed_cells, w_perm = lax.optimization_barrier((back_bf, out_rows, mixed_cells, w_perm))
-    grad_out_w = lax.all_to_all(out_rows, "col", 0, 1, tiled=True).reshape(e_dim // nc, c_dim)
+    unpair = lambda values: jnp.concatenate([values[0], values[1]], axis=-1)
+    returned = swap(jnp.concatenate([dact_across[..., :width], unpair(dproj_across)], axis=-1).astype(BF16))
+    returned, out_rows = exchange(
+        8, ("spread", "col", parts(returned, 1, nc)), ("gather", "row", out_sum)
+    )
+    returned = joined(returned, 0)
+    back_bf, w_perm, dact_across = lax.optimization_barrier((back_bf, w_perm, dact_across))
     dact_down, dproj_down = run_backward(
         act_down, proj_down, params_down, start_down, pad_to(back_bf, 2, lanes), pick, spread
     )
-    dproj_down, grad_out_w = lax.optimization_barrier((dproj_down, grad_out_w))
-    unpair = lambda values: jnp.concatenate([values[0], values[1]], axis=-1)
-    returned = lax.all_to_all(
-        swap(jnp.concatenate([dact_across[..., :width], unpair(dproj_across)], axis=-1).astype(BF16)),
-        "col", 1, 0, tiled=True,
-    )
     dproj = jnp.concatenate([unpair(dproj_down), returned[..., width:].astype(F32)], axis=-1)
-    dproj = lax.all_to_all(
-        dproj.astype(BF16).reshape(nr, rows, cols, dirs * coefs), "row", 0, 0, tiled=True
-    )
-    dproj = jnp.sum(dproj.astype(F32), axis=0)
-    dproj = lax.all_gather(dproj.astype(BF16), "row", axis=0, tiled=True)
+    dproj, out_own = exchange(
+        9, ("spread", "row", parts(dproj.astype(BF16), 0, nr)), ("spread", "col", parts(out_rows, 0, nc))
+    )
+    grad_out_w = jnp.swapaxes(out_own, 0, 1).reshape(e_dim // nc, c_dim)
+    dproj = jnp.sum(dproj.astype(F32), axis=0).astype(BF16)
+    (dproj,) = exchange(10, ("gather", "row", dproj))
     proj_rows = lax.dynamic_slice_in_dim(proj_weight, me * width, width, axis=0)
     back_active = lax.dot_general(
         dproj.reshape(-1, dirs * coefs), proj_rows, (((1,), (1,)), ((), ())), preferred_element_type=F32
@@ -458,7 +551,8 @@
     back_active = back_active + dact_down[..., :width] + returned[..., :width].astype(F32)
     conv_sig = jax.nn.sigmoid(convolved)
     back_conv = back_active * (conv_sig * (1.0 + convolved * (1.0 - conv_sig)))
-    grad_padded = col_halo(back_conv)
+    (conv_edges,) = exchange(11, ("halo", "col", edges(back_conv)))
+    grad_padded = with_edges(back_conv, conv_edges)
     back_source = jnp.zeros(source.shape, F32)
     for a in range(3):
         for b in range(3):
@@ -466,20 +560,22 @@
     back_xz = jnp.concatenate([back_source.astype(BF16), back_gate.astype(BF16)], axis=-1)
 
     result = field.astype(F32) + jnp.dot(mixed_cells, out_full, preferred_element_type=F32).reshape(field.shape)
-    xz_cells = lax.all_to_all(back_xz, "row", 0, 2, tiled=True).reshape(-1, 2 * e_dim)
+    in_part = lax.dot_general(
+        field_flat, back_xz.reshape(-1, 2 * width), contract, preferred_element_type=F32
+    )
+    xz_cells, in_parts = exchange(
+        12,
+        ("spread", "row", parts(back_xz, 0, nr)),
+        ("spread", "col", parts(in_part.astype(BF16), 0, nc)),
+    )
+    xz_cells = joined(xz_cells, 2).reshape(-1, 2 * e_dim)
+    in_sum = jnp.sum(in_parts.astype(F32), axis=0)
+    (in_piece,) = exchange(13, ("undeal", "row", parts(in_sum, 1, 2)))
+    (grad_in,) = exchange(14, ("gather", "col", jnp.concatenate([in_piece[0], in_piece[1]], axis=1)))
+    grad_in = grad_in.reshape(c_dim, 2 * width)
     grad_field = grad_out.astype(F32) + lax.dot_general(
         xz_cells, w_perm, (((1,), (1,)), ((), ())), preferred_element_type=F32
     ).reshape(field.shape)
-    in_part = lax.dot_general(
-        field_flat, back_xz.reshape(-1, 2 * width), contract, preferred_element_type=F32
-    )
-    in_sum = lax.psum(in_part, "col")
-    g_src, g_gate = in_sum[:, :width], in_sum[:, width:]
-    back_one = lax.ppermute(jnp.where(even, g_src, g_gate), "row", reverse_moves(moves_one))
-    back_two = lax.ppermute(jnp.where(even, g_gate, g_src), "row", reverse_moves(moves_two))
-    grad_in = jnp.concatenate(
-        [jnp.where(low, back_one, back_two), jnp.where(low, back_two, back_one)], axis=1
-    )
     return (result.astype(BF16), grad_field, grad_in, grad_out_w.astype(F32))
 
 

time: 392 us -> 360 us (0.918)
  Pallas kernels: 105 us -> 263 us
  waiting for transfers between devices: 102 us -> 0.75 us
  blocking collectives: 59.4 us -> 0 us
  starting transfers between devices: 45.8 us -> 0.12 us
  local copies, waits for them, and re-layouts: 20.6 us -> 42.4 us
  other arithmetic: 31.4 us -> 25.8 us
    pallas_call x0 -> x15, Pallas kernels: none -> 158 us  [exchange(): pl.pallas_call(lambda *refs: exchange_kernel(plan, sizes, *refs), in_spec...]
    all_gather x4 -> x0, blocking collectives: 37.7 us -> none  [the longest x1 10.6 us: local(): out_rows = lax.all_gather(out_sum.astype(BF16), 'row', axis=0)]
    all_to_all x7 -> x0, starting transfers between devices: 28.5 us -> none  [the longest x1 5.09 us: local(): lax.all_to_all(swap(jnp.concatenate([dact_across[..., :width], unpair(dpr...]
    all_to_all x7 -> x0, waiting for transfers between devices: 25.1 us -> none  [the longest x1 14.4 us: local(): lax.all_to_all(jnp.concatenate([active, proj[..., split:]], axis=-1), 'co...]
    all_to_all x2 -> x0, blocking collectives: 21.8 us -> none  [the longest x1 12.3 us: local(): lax.all_to_all(dproj.astype(BF16).reshape(nr, rows, cols, dirs * coefs),...]
    psum x1 -> x0, waiting for transfers between devices: 20.8 us -> none  [local(): in_sum = lax.psum(in_part, 'col')]
    ppermute x8 -> x0, waiting for transfers between devices: 19.4 us -> none  [the longest x2 8.23 us: col_halo(): before = lax.ppermute(cells[:, -1:], 'col', up)]
    ppermute x8 -> x0, starting transfers between devices: 17.2 us -> none  [the longest x2 7.26 us: col_halo(): after = lax.ppermute(cells[:, :1], 'col', down)]
  transfers between devices with their start and end apart: 21 -> 3, of which waited for: 13 -> 0; matrix products, arithmetic and copies ran while one was open for 11% -> 16% of each run, Pallas kernels for 27% -> 49%
where the time goes in v2:
time: 360 us; the launch traced here: 358 us
  Pallas kernels  263 us (73%)
  local copies, waits for them, and re-layouts  42.4 us (12%)
  other arithmetic  25.8 us (7%)
  between operations  14.3 us (4%)
  matrix products  11.1 us (3%)
    pallas_call x15, Pallas kernels, exchange(): pl.pallas_call(lambda *refs: exchange_kernel(plan, sizes, *refs), in_spec...  158 us
    pallas_call x2, Pallas kernels, run_backward(): pl.pallas_call(lambda *refs: backward_kernel(states, *refs), grid=(2,), i...  69.7 us
    pallas_call x2, Pallas kernels, run_forward(): pl.pallas_call(lambda *refs: forward_kernel(states, *refs), grid=(2,), in...  35.3 us
  transfers between devices with their start and end apart: 3, of which 0 were waited for; matrix products, arithmetic and copies ran while one was open for 16% of the time, Pallas kernels for 49%

profile of v2, /device:TPU:0, one launch (start us, length us, event | category | flops | bytes accessed | tf_op | source)
XLA Modules:
  0.0 357.6 jit_solution(13320041668541644389)
XLA Ops:
  11.7 20.1 %exchange_0.1 = (bf16[2,512,128]{2,1,0:T(8,128)(2,1)}, bf16[8,8,16,512]{3,2,1,0:T(8,128)(2,1)}) custom-call(bf16[2,512,128]{2,1,0:T(8,128)(2,1)} %bitcast.205, bf16[8,16,512]{2,1,0:T(8,128)(2,1)} %refs_1_.1), custom_call_target="tpu_custom_call" | custom-call | tf_op jit(solution)/shard_map/exchange_0/pallas_call | solution.py:375
  36.0 6.6 %exchange_1.1 = bf16[2,64,128]{2,1,0:T(8,128)(2,1)} custom-call(bf16[2,64,128]{2,1,0:T(8,128)(2,1)} %pad_maximum_fusion.20.refs_0_), custom_call_target="tpu_custom_call" | custom-call | tf_op jit(solution)/shard_map/exchange_1/pallas_call | solution.py:375
  48.5 12.5 %exchange_2.1 = (bf16[8,8,16,128]{3,2,1,0:T(8,128)(2,1)}, bf16[4,16,16,128]{3,2,1,0:T(8,128)(2,1)}) custom-call(bf16[8,8,16,128]{3,2,1,0:T(8,128)(2,1)} %copy.145.refs_0_, bf16[4,16,16,128]{3,2,1,0:T(8,128)(2,1)} %copy.146.refs_1_), custom_call_target="tpu_custom_call" | custom-call | tf_op jit(solution)/shard_map/exchange_2/pallas_call | solution.py:375
  63.0 9.2 %exchange_3.1 = bf16[8,8,16,256]{3,2,1,0:T(8,128)(2,1)} custom-call(bf16[8,16,256]{2,1,0:T(8,128)(2,1)} %bitcast.226), custom_call_target="tpu_custom_call" | custom-call | tf_op jit(solution)/shard_map/exchange_3/pallas_call | solution.py:375
  76.0 2.7 fusion.2.refs_9_
  79.5 12.1 %exchange_4.1 = bf16[4,16,16,128]{3,2,1,0:T(8,128)(2,1)} custom-call(bf16[4,16,16,128]{3,2,1,0:T(8,128)(2,1)} %bitcast.202), custom_call_target="tpu_custom_call" | custom-call | tf_op jit(solution)/shard_map/exchange_4/pallas_call | solution.py:375
  98.7 17.6 %scan_forward.3 = (f32[64,16,128]{2,1,0:T(8,128)}, f32[2,16,16,128]{3,2,1,0:T(8,128)}) custom-call(bf16[64,16,128]{2,1,0:T(8,128)(2,1)} %bitcast.220, bf16[2,64,16,64]{3,2,1,0:T(8,128)(2,1)} %pad_maximum_fusion.7.refs_1_, bf16[2,64,128]{2,1,0:T(8,128)(2,1)} %copy.153.refs_2_, f32[2,8,128]{2,1,0:T(8,128)} %broadcast_in_dim.55.refs_3_.refs_4_, ...), custom_call_target="tpu_custom_call" | custom-call | flops 83886080 | bytes 2097152 | tf_op jit(solution)/shard_map/scan_forward/pallas_call | solution.py:219
  118.2 9.6 %exchange_5.1 = bf16[4,16,16,128]{3,2,1,0:T(8,128)(2,1)} custom-call(bf16[4,16,16,128]{3,2,1,0:T(8,128)(2,1)} %bitcast.208), custom_call_target="tpu_custom_call" | custom-call | tf_op jit(solution)/shard_map/exchange_5/pallas_call | solution.py:375
  133.1 17.6 %scan_forward.2 = (f32[64,16,128]{2,1,0:T(8,128)}, f32[2,16,16,128]{3,2,1,0:T(8,128)}) custom-call(bf16[64,16,128]{2,1,0:T(8,128)(2,1)} %copy.149.refs_0_, bf16[2,64,16,64]{3,2,1,0:T(8,128)(2,1)} %pad_maximum_fusion.6.refs_1_, bf16[2,64,128]{2,1,0:T(8,128)(2,1)} %copy.150.refs_2_, f32[2,8,128]{2,1,0:T(8,128)} %broadcast_in_dim.24.refs_3_.refs_4_, ...), custom_call_target="tpu_custom_call" | custom-call | flops 83886080 | bytes 2097152 | tf_op jit(solution)/shard_map/scan_forward/pallas_call | solution.py:219
  152.7 1.8 copy.159
  158.0 5.6 %exchange_6.1 = f32[8,32,128]{2,1,0:T(8,128)} custom-call(f32[32,128]{1,0:T(8,128)} %reshape.179.refs_0_), custom_call_target="tpu_custom_call" | custom-call | tf_op jit(solution)/shard_map/exchange_6/pallas_call | solution.py:375
  165.4 1.9 fusion.20
  170.1 13.8 %exchange_7.1 = (bf16[4,16,16,128]{3,2,1,0:T(8,128)(2,1)}, bf16[8,8,16,128]{3,2,1,0:T(8,128)(2,1)}, bf16[4,32,512]{2,1,0:T(8,128)(2,1)}) custom-call(bf16[4,16,16,128]{3,2,1,0:T(8,128)(2,1)} %copy.171.refs_0_, bf16[8,8,16,128]{3,2,1,0:T(8,128)(2,1)} %copy.172.refs_1_, bf16[4,32,512]{2,1,0:T(8,128)(2,1)} %bitcast.217), custom_call_target="tpu_custom_call" | custom-call | tf_op jit(solution)/shard_map/exchange_7/pallas_call | solution.py:375
  185.6 34.9 %scan_backward.2 = (f32[64,16,128]{2,1,0:T(8,128)}, f32[2,64,16,64]{3,2,1,0:T(8,128)}) custom-call(bf16[64,16,128]{2,1,0:T(8,128)(2,1)} %bitcast.221, bf16[2,64,16,64]{3,2,1,0:T(8,128)(2,1)} %pad_maximum_fusion.7.refs_1_, bf16[2,64,128]{2,1,0:T(8,128)(2,1)} %copy.153.refs_2_, bf16[2,128,64]{2,1,0:T(8,128)(2,1)} %get-tuple-element.90.refs_3_, ...), custom_call_target="tpu_custom_call" | custom-call | flops 125829120 | bytes 4194304 | tf_op jit(solution)/shard_map/scan_backward/pallas_call | solution.py:251
  224.7 13.9 %exchange_8.1 = (bf16[4,16,16,256]{3,2,1,0:T(8,128)(2,1)}, bf16[8,32,512]{2,1,0:T(8,128)(2,1)}) custom-call(bf16[4,16,16,256]{3,2,1,0:T(8,128)(2,1)} %bitcast.194, bf16[32,512]{1,0:T(8,128)(2,1)} %reduce_sum.123.refs_1_), custom_call_target="tpu_custom_call" | custom-call | tf_op jit(solution)/shard_map/exchange_8/pallas_call | solution.py:375
  240.1 1.9 fusion.9
  242.9 34.9 %scan_backward.3 = (f32[64,16,128]{2,1,0:T(8,128)}, f32[2,64,16,64]{3,2,1,0:T(8,128)}) custom-call(bf16[64,16,128]{2,1,0:T(8,128)(2,1)} %copy.149.refs_0_, bf16[2,64,16,64]{3,2,1,0:T(8,128)(2,1)} %pad_maximum_fusion.6.refs_1_, bf16[2,64,128]{2,1,0:T(8,128)(2,1)} %copy.150.refs_2_, bf16[2,128,64]{2,1,0:T(8,128)(2,1)} %get-tuple-element.89.refs_3_, ...), custom_call_target="tpu_custom_call" | custom-call | flops 125829120 | bytes 4194304 | tf_op jit(solution)/shard_map/scan_backward/pallas_call | solution.py:251
  280.1 10.1 %exchange_9.1 = (bf16[8,8,16,256]{3,2,1,0:T(8,128)(2,1)}, bf16[4,2,32,512]{3,2,1,0:T(8,128)(2,1)}) custom-call(bf16[8,8,16,256]{3,2,1,0:T(8,128)(2,1)} %pad_maximum_fusion.9.refs_0_, bf16[4,2,32,512]{3,2,1,0:T(8,128)(2,1)} %bitcast.218), custom_call_target="tpu_custom_call" | custom-call | tf_op jit(solution)/shard_map/exchange_9/pallas_call | solution.py:375
  290.2 1.8 reduce_sum.124.refs_0_
  291.9 9.3 %exchange_10.1 = bf16[8,8,16,256]{3,2,1,0:T(8,128)(2,1)} custom-call(bf16[8,16,256]{2,1,0:T(8,128)(2,1)} %reduce_sum.124.refs_0_), custom_call_target="tpu_custom_call" | custom-call | tf_op jit(solution)/shard_map/exchange_10/pallas_call | solution.py:375
  303.5 6.3 %exchange_11.1 = f32[2,64,128]{2,1,0:T(8,128)} custom-call(f32[2,64,128]{2,1,0:T(8,128)} %pad_maximum_fusion.19.refs_0_), custom_call_target="tpu_custom_call" | custom-call | tf_op jit(solution)/shard_map/exchange_11/pallas_call | solution.py:375
  313.1 10.9 %exchange_12.1 = (bf16[8,8,16,256]{3,2,1,0:T(8,128)(2,1)}, bf16[4,128,256]{2,1,0:T(8,128)(2,1)}) custom-call(bf16[8,8,16,256]{3,2,1,0:T(8,128)(2,1)} %bitcast.196, bf16[4,128,256]{2,1,0:T(8,128)(2,1)} %bitcast.219), custom_call_target="tpu_custom_call" | custom-call | tf_op jit(solution)/shard_map/exchange_12/pallas_call | solution.py:375
  327.1 4.9 %exchange_13.1 = f32[2,128,128]{2,1,0:T(8,128)} custom-call(f32[2,128,128]{2,1,0:T(8,128)} %bitcast.216), custom_call_target="tpu_custom_call" | custom-call | tf_op jit(solution)/shard_map/exchange_13/pallas_call | solution.py:375
  333.5 13.4 %exchange_14.1 = f32[4,128,256]{2,1,0:T(8,128)} custom-call(f32[128,256]{1,0:T(8,128)} %pad_maximum_fusion.18.refs_0_), custom_call_target="tpu_custom_call" | custom-call | tf_op jit(solution)/shard_map/exchange_14/pallas_call | solution.py:375
  (143 shorter events, 70.1 us)
Async XLA Ops:
  7.2 55.0 %copy-start = (bf16[1024,256]{1,0:T(8,128)(2,1)S(1)}, bf16[1024,256]{1,0:T(8,128)(2,1)}, u32[]{:S(2)}) copy-start(bf16[1024,256]{1,0:T(8,128)(2,1)} %param.14) | copy-start | bytes 1572868
  7.2 145.5 %all-gather.6.cloned.1.call-start = ((), (), s32[]{:S(2)}) async-start(), calls=%async_computation.1 | async-start | bytes 1179648 | tf_op jit(solution)/shard_map/all_gather | solution.py:433
  8.9 145.6 %all-gather.4.cloned.1.call-start = ((), (), s32[]{:S(2)}) async-start(), calls=%async_computation | async-start | bytes 1310720 | tf_op jit(solution)/shard_map/all_gather | solution.py:434
  9.7 232.3 %all-gather.8.cloned.1.call-start = ((), (), s32[]{:S(2)}) async-start(), calls=%async_computation.2 | async-start | bytes 2359296 | tf_op jit(solution)/shard_map/all_gather | solution.py:435
  63.0 15.7 %copy-start.9 = (bf16[4,16,16,128]{3,2,1,0:T(8,128)(2,1)S(1)}, bf16[4,16,16,128]{3,2,1,0:T(8,128)(2,1)}, u32[]{:S(2)}) copy-start(bf16[4,16,16,128]{3,2,1,0:T(8,128)(2,1)} %get-tuple-element.31) | copy-start | bytes 786436
  165.2 3.9 %copy-start.1 = (bf16[64,16,512]{2,0,1:T(8,128)(2,1)S(1)}, bf16[64,16,512]{2,0,1:T(8,128)(2,1)}, u32[]{:S(2)}) copy-start(bf16[64,16,512]{2,0,1:T(8,128)(2,1)} %all-gather.6.cloned.1.call-done) | copy-start | bytes 3145732
  221.7 2.3 copy-start.10
  223.1 17.0 %copy-start.5 = (bf16[1024,512]{1,0:T(8,128)(2,1)S(1)}, bf16[1024,512]{1,0:T(8,128)(2,1)}, u32[]{:S(2)}) copy-start(bf16[1024,512]{1,0:T(8,128)(2,1)} %all-gather.4.cloned.1.call-done) | copy-start | bytes 3145732
  223.1 17.0 %copy-start.6 = (bf16[8,16,512]{2,1,0:T(8,128)(2,1)S(1)}, bf16[8,16,512]{2,1,0:T(8,128)(2,1)}, u32[]{:S(2)}) copy-start(bf16[8,16,512]{2,1,0:T(8,128)(2,1)} %refs_1_.1) | copy-start | bytes 393220
  279.0 22.2 %copy-start.8 = (f32[64,16,128]{2,0,1:T(8,128)S(1)}, f32[64,16,128]{2,0,1:T(8,128)}, u32[]{:S(2)}) copy-start(f32[64,16,128]{2,0,1:T(8,128)} %get-tuple-element.63) | copy-start | bytes 1572868
  279.0 22.2 %copy-start.12 = (f32[64,16,128]{2,1,0:T(8,128)S(1)}, f32[64,16,128]{2,1,0:T(8,128)}, u32[]{:S(2)}) copy-start(f32[64,16,128]{2,1,0:T(8,128)} %get-tuple-element.45) | copy-start | bytes 1572868
  310.6 1.2 copy-start.11
  311.4 1.7 copy-start.4
  325.1 23.7 %copy-start.3 = (bf16[512,2048]{1,0:T(8,128)(2,1)S(1)}, bf16[512,2048]{1,0:T(8,128)(2,1)}, u32[]{:S(2)}) copy-start(bf16[512,2048]{1,0:T(8,128)(2,1)} %all-gather.8.cloned.1.call-done) | copy-start | bytes 6291460
  325.1 23.7 %copy-start.7 = (bf16[8,16,512]{2,1,0:T(8,128)(2,1)S(1)}, bf16[8,16,512]{2,1,0:T(8,128)(2,1)}, u32[]{:S(2)}) copy-start(bf16[8,16,512]{2,1,0:T(8,128)(2,1)} %param.21) | copy-start | bytes 393220
  347.9 2.4 copy-start.2
Sparse Core Ops, SparseCore 0:
  10.5 32.5 all-gather.5
  44.6 31.3 all-gather.3
  77.9 27.3 all-gather.7

commit v3 on v2

--- a/solution.py
+++ b/solution.py
@@ -59,12 +59,25 @@
 
 def forward_kernel(
     states, act_ref, proj_ref, dtw_ref, bias_ref, rate_ref, skip_ref, spread_ref, y_ref, start_ref, step_ref, wide_ref,
+    wide_rate, *kept,
 ):
     k = pl.program_id(0)
     length, lines, width = act_ref.shape
     fill_steps(proj_ref, dtw_ref, bias_ref, None, step_ref)
     spread_coefs(proj_ref, spread_ref, wide_ref)
+    for n in range(states):
+        wide_rate[n] = jnp.broadcast_to(rate_ref[n : n + 1, :], (lines, width))
+    rate_ref = wide_rate
     zero = jnp.zeros((lines, width), F32)
+
+    def make_decay(i, n, step):
+        decay = jnp.exp2(step * rate_ref[n])
+        if kept:
+            kept[0][i, n] = decay
+        return decay
+
+    def decay_at(i, n, step):
+        return kept[0][i, n] if kept else jnp.exp2(step * rate_ref[n])
 
     def place(i):
         return jnp.where(k == 0, i, length - 1 - i)
@@ -78,7 +91,7 @@
         step = step_ref[p]
         drive = step * act_ref[p].astype(F32)
         state = tuple(
-            jnp.exp2(step * rate_ref[n]) * state[n] + drive * coef(p, n) for n in range(states)
+            make_decay(i, n, step) * state[n] + drive * coef(p, n) for n in range(states)
         )
         return state, total + step
 
@@ -103,7 +116,7 @@
         y = y_ref[p] + skip * act
         new = []
         for n in range(states):
-            one = jnp.exp2(step * rate_ref[n]) * state[n] + drive * coef(p, n)
+            one = decay_at(i, n, step) * state[n] + drive * coef(p, n)
             y = y + one * coef(p, states + n)
             new.append(one)
         y_ref[p] = y
@@ -115,12 +128,25 @@
 def backward_kernel(
     states, act_ref, proj_ref, dtw_ref, dtwt_ref, bias_ref, rate_ref, skip_ref, start_ref, gy_ref, pick_ref, spread_ref,
     dact_ref, dproj_ref, raw_ref, step_ref, h_ref, wide_ref, prod_ref, draw_ref,
+    wide_rate, *kept,
 ):
     k = pl.program_id(0)
     length, lines, width = act_ref.shape
     fill_steps(proj_ref, dtw_ref, bias_ref, raw_ref, step_ref)
     spread_coefs(proj_ref, spread_ref, wide_ref)
+    for n in range(states):
+        wide_rate[n] = jnp.broadcast_to(rate_ref[n : n + 1, :], (lines, width))
+    rate_ref = wide_rate
     zero = jnp.zeros((lines, width), F32)
+
+    def make_decay(i, n, step):
+        decay = jnp.exp2(step * rate_ref[n])
+        if kept:
+            kept[0][i, n] = decay
+        return decay
+
+    def decay_at(i, n, step):
+        return kept[0][i, n] if kept else jnp.exp2(step * rate_ref[n])
 
     def place(i):
         return jnp.where(k == 0, i, length - 1 - i)
@@ -138,7 +164,7 @@
         drive = step * act_ref[p].astype(F32)
         new = []
         for n in range(states):
-            one = jnp.exp2(step * rate_ref[n]) * state[n] + drive * coef(p, n)
+            one = make_decay(i, n, step) * state[n] + drive * coef(p, n)
             h_ref[i + 1, n] = one.astype(BF16)
             new.append(one)
         return tuple(new), total + step
@@ -146,11 +172,12 @@
     _, total = loop(length, replay, (tuple(start_ref[n] for n in range(states)), zero), 2)
 
     def adjoint(j, back):
-        p = place(length - 1 - j)
+        i = length - 1 - j
+        p = place(i)
         gy = gy_ref[p].astype(F32)
         step = step_ref[p]
         return tuple(
-            jnp.exp2(step * rate_ref[n]) * (back[n] + gy * coef(p, states + n)) for n in range(states)
+            decay_at(i, n, step) * (back[n] + gy * coef(p, states + n)) for n in range(states)
         )
 
     back = loop(length, adjoint, (zero,) * states, 2)
@@ -182,7 +209,7 @@
                 prod_ref[q, :, pl.ds(n * width, width)] = (drive * lam).astype(BF16)
                 prod_ref[q, :, pl.ds((states + n) * width, width)] = (gy * h_ref[i + 1, n].astype(F32)).astype(BF16)
                 ddrive = ddrive + lam * coef(p, n)
-                carried = jnp.exp2(step * rate) * lam
+                carried = decay_at(i, n, step) * lam
                 dstep = dstep + (carried * h_ref[i, n].astype(F32)) * rate
                 new.append(carried)
             dstep = LN2 * dstep + act * ddrive
@@ -207,13 +234,19 @@
     return pl.BlockSpec(shape, lambda k: (0,) * len(shape))
 
 
-def each_spec(shape):
-    return pl.BlockSpec((None,) + shape, lambda k: (k,) + (0,) * len(shape))
+def each_spec(shape, first=0):
+    return pl.BlockSpec((None,) + shape, lambda k: (first + k,) + (0,) * len(shape))
+
+
+def decay_room(length, states, lines, width, taken):
+    size = length * states * lines * width
+    return [pltpu.VMEM((length, states, lines, width), F32)] if 4 * size + taken <= 48 * 2**20 else []
 
 
 def run_forward(act, proj, params, spread):
-    dtw, dtwt, bias, rates, skip, rank, states = params
+    dtw, dtwt, bias, rates, skip, states, first = params
     length, lines, width = act.shape
+    big = length * lines * 2 * states * width
     coefs = proj.shape[-1]
     work = 2 * 2 * length * lines * width * states
     return pl.pallas_call(
@@ -222,10 +255,10 @@
         in_specs=[
             whole_spec(act.shape),
             each_spec((length, lines, coefs)),
-            each_spec((coefs, width)),
-            each_spec((8, width)),
-            each_spec((states, lines, width)),
-            each_spec((8, width)),
+            each_spec((coefs, width), first),
+            each_spec((8, width), first),
+            each_spec((states, width), first),
+            each_spec((8, width), first),
             whole_spec(spread.shape),
         ],
         out_specs=[whole_spec(act.shape), each_spec((states, lines, width))],
@@ -236,7 +269,9 @@
         scratch_shapes=[
             pltpu.VMEM(act.shape, F32),
             pltpu.VMEM((length, lines, 2 * states * width), F32),
-        ],
+            pltpu.VMEM((states, lines, width), F32),
+        ]
+        + decay_room(length, states, lines, width, 4 * big),
         compiler_params=pltpu.CompilerParams(vmem_limit_bytes=56 * 2**20),
         cost_estimate=pl.CostEstimate(flops=10 * work, bytes_accessed=4 * act.size * 4, transcendentals=work),
         name="scan_forward",
@@ -244,8 +279,9 @@
 
 
 def run_backward(act, proj, params, start, gy, pick, spread):
-    dtw, dtwt, bias, rates, skip, rank, states = params
+    dtw, dtwt, bias, rates, skip, states, first = params
     length, lines, width = act.shape
+    big = length * lines * 2 * states * width
     coefs = proj.shape[-1]
     work = 2 * 3 * length * lines * width * states
     return pl.pallas_call(
@@ -254,11 +290,11 @@
         in_specs=[
             whole_spec(act.shape),
             each_spec((length, lines, coefs)),
-            each_spec((coefs, width)),
-            each_spec((width, coefs)),
-            each_spec((8, width)),
-            each_spec((states, lines, width)),
-            each_spec((8, width)),
+            each_spec((coefs, width), first),
+            each_spec((width, coefs), first),
+            each_spec((8, width), first),
+            each_spec((states, width), first),
+            each_spec((8, width), first),
             each_spec((states, lines, width)),
             whole_spec(act.shape),
             whole_spec(pick.shape),
@@ -276,7 +312,9 @@
             pltpu.VMEM((length, lines, 2 * states * width), F32),
             pltpu.VMEM((8, lines, 2 * states * width), BF16),
             pltpu.VMEM((8, lines, width), BF16),
-        ],
+            pltpu.VMEM((states, lines, width), F32),
+        ]
+        + decay_room(length, states, lines, width, 5 * big),
         compiler_params=pltpu.CompilerParams(vmem_limit_bytes=60 * 2**20),
         cost_estimate=pl.CostEstimate(flops=10 * work, bytes_accessed=8 * act.size * 4, transcendentals=work),
         name="scan_backward",
@@ -430,10 +468,6 @@
     field_flat = field_all.reshape(-1, c_dim)
     xz = jnp.dot(field_flat, w_mine, preferred_element_type=F32).astype(BF16).reshape(all_rows, cols, 2 * width)
     source, gate = xz[..., :width], xz[..., width:].astype(F32)
-    grad_all = lax.all_gather(grad_out, "row", axis=0, tiled=True)
-    out_full = lax.all_gather(out_weight, "col", axis=0, tiled=True)
-    w_perm = lax.all_gather(w_mine, "row", axis=1, tiled=True)
-
     taps = mine(conv_weight)
     (source_edges,) = exchange(1, ("halo", "col", edges(source)))
     padded = with_edges(source, source_edges)
@@ -454,6 +488,10 @@
     (proj_col,) = exchange(4, ("spread", "col", parts(proj[..., split:], 0, nc)))
     act_down = active
     act_across, across = swap(joined(act_col, 1)), swap(joined(proj_col, 1))
+    act_across, later_grad, later_out, later_w = lax.optimization_barrier((act_across, grad_out, out_weight, w_mine))
+    grad_all = lax.all_gather(later_grad, "row", axis=0, tiled=True)
+    out_full = lax.all_gather(later_out, "col", axis=0, tiled=True)
+    w_perm = lax.all_gather(later_w, "row", axis=1, tiled=True)
     pair = lambda values: jnp.stack([values[..., :coefs], values[..., coefs:]], axis=0)
     proj_down, proj_across = pair(proj[..., :split]), pair(across)
 
@@ -465,20 +503,16 @@
     rates = -LOG2E * pad_to(mine(decay_rate), 2, lanes, 1.0)
     skip = jnp.broadcast_to(pad_to(mine(skip_gain), 1, lanes)[:, None, :], (dirs, 8, lanes))
 
-    def params(at, count):
-        wide = jnp.broadcast_to(rates[at : at + 2][:, :, None, :], (2, states, count, lanes))
-        cut = slice(at, at + 2)
-        return dtw[cut], dtwt[cut], bias[cut], wide, skip[cut], rank, states
-
-    params_down, params_across = params(0, act_down.shape[1]), params(2, act_across.shape[1])
+    params_down = (dtw, dtwt, bias, rates, skip, states, 0)
+    params_across = (dtw, dtwt, bias, rates, skip, states, 2)
     act_down, act_across = pad_to(act_down, 2, lanes), pad_to(act_across, 2, lanes)
     spots = jnp.repeat(jnp.arange(2 * states) + rank, lanes)
     pick = (spots[:, None] == jnp.arange(coefs)[None, :]).astype(BF16)
     spread = pick.T
     y_across, start_across = run_forward(act_across, proj_across, params_across, spread)
     y_down, start_down = run_forward(act_down, proj_down, params_down, spread)
-    (y_back,) = exchange(5, ("spread", "col", parts(swap(y_across[..., :width].astype(BF16)), 1, nc)))
-    summed = y_down[..., :width] + joined(y_back, 0).astype(F32)
+    y_back = lax.all_to_all(swap(y_across[..., :width].astype(BF16)), "col", 1, 0, tiled=True)
+    summed = y_down[..., :width] + y_back.astype(F32)
 
     back_mixed = lax.dot_general(
         grad_all.reshape(-1, c_dim),
@@ -529,21 +563,18 @@
     )
     unpair = lambda values: jnp.concatenate([values[0], values[1]], axis=-1)
     returned = swap(jnp.concatenate([dact_across[..., :width], unpair(dproj_across)], axis=-1).astype(BF16))
-    returned, out_rows = exchange(
-        8, ("spread", "col", parts(returned, 1, nc)), ("gather", "row", out_sum)
-    )
-    returned = joined(returned, 0)
+    returned = lax.all_to_all(returned, "col", 1, 0, tiled=True)
     back_bf, w_perm, dact_across = lax.optimization_barrier((back_bf, w_perm, dact_across))
     dact_down, dproj_down = run_backward(
         act_down, proj_down, params_down, start_down, pad_to(back_bf, 2, lanes), pick, spread
     )
     dproj = jnp.concatenate([unpair(dproj_down), returned[..., width:].astype(F32)], axis=-1)
-    dproj, out_own = exchange(
-        9, ("spread", "row", parts(dproj.astype(BF16), 0, nr)), ("spread", "col", parts(out_rows, 0, nc))
-    )
+    dproj, out_rows = exchange(
+        9, ("spread", "row", parts(dproj.astype(BF16), 0, nr)), ("gather", "row", out_sum)
+    )
+    dproj = jnp.sum(dproj.astype(F32), axis=0).astype(BF16)
+    dproj, out_own = exchange(10, ("gather", "row", dproj), ("spread", "col", parts(out_rows, 0, nc)))
     grad_out_w = jnp.swapaxes(out_own, 0, 1).reshape(e_dim // nc, c_dim)
-    dproj = jnp.sum(dproj.astype(F32), axis=0).astype(BF16)
-    (dproj,) = exchange(10, ("gather", "row", dproj))
     proj_rows = lax.dynamic_slice_in_dim(proj_weight, me * width, width, axis=0)
     back_active = lax.dot_general(
         dproj.reshape(-1, dirs * coefs), proj_rows, (((1,), (1,)), ((), ())), preferred_element_type=F32
@@ -570,9 +601,9 @@
     )
     xz_cells = joined(xz_cells, 2).reshape(-1, 2 * e_dim)
     in_sum = jnp.sum(in_parts.astype(F32), axis=0)
-    (in_piece,) = exchange(13, ("undeal", "row", parts(in_sum, 1, 2)))
+    (in_piece,) = exchange(13, ("undeal", "row", parts(in_sum.astype(BF16), 1, 2)))
     (grad_in,) = exchange(14, ("gather", "col", jnp.concatenate([in_piece[0], in_piece[1]], axis=1)))
-    grad_in = grad_in.reshape(c_dim, 2 * width)
+    grad_in = grad_in.reshape(c_dim, 2 * width).astype(F32)
     grad_field = grad_out.astype(F32) + lax.dot_general(
         xz_cells, w_perm, (((1,), (1,)), ((), ())), preferred_element_type=F32
     ).reshape(field.shape)

time: 360 us -> 344 us (0.956)
  Pallas kernels: 263 us -> 228 us
  waiting for transfers between devices: 0.75 us -> 13.5 us
  starting transfers between devices: 0.12 us -> 11.8 us
  local copies, waits for them, and re-layouts: 42.4 us -> 33 us
    pallas_call x15 -> x13, Pallas kernels: 158 us -> 129 us  [exchange(): pl.pallas_call(lambda *refs: exchange_kernel(plan, sizes, *refs), in_spec...]
    all_to_all x0 -> x2, waiting for transfers between devices: none -> 12.1 us  [the longest x1 12.1 us: local(): returned = lax.all_to_all(returned, 'col', 1, 0, tiled=True)]
    all_to_all x0 -> x2, starting transfers between devices: none -> 11.8 us  [the longest x1 8.06 us: local(): lax.all_to_all(swap(y_across[..., :width].astype(BF16)), 'col', 1, 0, til...]
    pallas_call x2, Pallas kernels: 69.7 us -> 65.3 us  [run_backward(): pl.pallas_call(lambda *refs: backward_kernel(states, *refs), grid=(2,), i...]
  transfers between devices with their start and end apart: 3 -> 5, of which waited for: 0 -> 1; matrix products, arithmetic and copies ran while one was open for 16% -> 12% of each run, Pallas kernels for 49% -> 32%
where the time goes in v3:
time: 344 us; the launch traced here: 343 us
  Pallas kernels  228 us (66%)
  local copies, waits for them, and re-layouts  33 us (10%)
  other arithmetic  28.8 us (8%)
  between operations  14.5 us (4%)
  waiting for transfers between devices  13.5 us (4%)
  matrix products  13.1 us (4%)
  starting transfers between devices  11.8 us (3%)
    pallas_call x13, Pallas kernels, exchange(): pl.pallas_call(lambda *refs: exchange_kernel(plan, sizes, *refs), in_spec...  129 us
    pallas_call x2, Pallas kernels, run_backward(): pl.pallas_call(lambda *refs: backward_kernel(states, *refs), grid=(2,), i...  65.3 us
    pallas_call x2, Pallas kernels, run_forward(): pl.pallas_call(lambda *refs: forward_kernel(states, *refs), grid=(2,), in...  33.3 us
    all_to_all x1, waiting for transfers between devices, local(): returned = lax.all_to_all(returned, 'col', 1, 0, tiled=True)  12.1 us
    all_to_all x1, starting transfers between devices, local(): lax.all_to_all(swap(y_across[..., :width].astype(BF16)), 'col', 1, 0, til...  8.06 us
  transfers between devices with their start and end apart: 5, of which 1 were waited for; matrix products, arithmetic and copies ran while one was open for 12% of the time, Pallas kernels for 32%

profile of v3, /device:TPU:0, one launch (start us, length us, event | category | flops | bytes accessed | tf_op | source)
XLA Modules:
  0.0 342.5 jit_solution(6755059873804742339)
XLA Ops:
  9.2 18.7 %exchange_0.1 = (bf16[2,512,128]{2,1,0:T(8,128)(2,1)}, bf16[8,8,16,512]{3,2,1,0:T(8,128)(2,1)}) custom-call(bf16[2,512,128]{2,1,0:T(8,128)(2,1)} %bitcast.199, bf16[8,16,512]{2,1,0:T(8,128)(2,1)} %refs_1_.1), custom_call_target="tpu_custom_call" | custom-call | tf_op jit(solution)/shard_map/exchange_0/pallas_call | solution.py:413
  32.1 6.6 %exchange_1.1 = bf16[2,64,128]{2,1,0:T(8,128)(2,1)} custom-call(bf16[2,64,128]{2,1,0:T(8,128)(2,1)} %pad_maximum_fusion.19.refs_0_), custom_call_target="tpu_custom_call" | custom-call | tf_op jit(solution)/shard_map/exchange_1/pallas_call | solution.py:413
  43.7 10.0 %exchange_2.1 = (bf16[8,8,16,128]{3,2,1,0:T(8,128)(2,1)}, bf16[4,16,16,128]{3,2,1,0:T(8,128)(2,1)}) custom-call(bf16[8,8,16,128]{3,2,1,0:T(8,128)(2,1)} %copy.135.refs_0_, bf16[4,16,16,128]{3,2,1,0:T(8,128)(2,1)} %copy.136.refs_1_), custom_call_target="tpu_custom_call" | custom-call | tf_op jit(solution)/shard_map/exchange_2/pallas_call | solution.py:413
  58.3 9.2 %exchange_3.1 = bf16[8,8,16,256]{3,2,1,0:T(8,128)(2,1)} custom-call(bf16[8,16,256]{2,1,0:T(8,128)(2,1)} %bitcast.219), custom_call_target="tpu_custom_call" | custom-call | tf_op jit(solution)/shard_map/exchange_3/pallas_call | solution.py:413
  69.2 13.2 %exchange_4.1 = bf16[4,16,16,128]{3,2,1,0:T(8,128)(2,1)} custom-call(bf16[4,16,16,128]{3,2,1,0:T(8,128)(2,1)} %bitcast.203), custom_call_target="tpu_custom_call" | custom-call | tf_op jit(solution)/shard_map/exchange_4/pallas_call | solution.py:413
  90.3 16.6 %scan_forward.3 = (f32[64,16,128]{2,1,0:T(8,128)}, f32[2,16,16,128]{3,2,1,0:T(8,128)}) custom-call(bf16[64,16,128]{2,1,0:T(8,128)(2,1)} %bitcast.211, bf16[2,64,16,64]{3,2,1,0:T(8,128)(2,1)} %pad_maximum_fusion.7.refs_1_, bf16[4,64,128]{2,1,0:T(8,128)(2,1)} %pad.4.clone.refs_2_, f32[4,8,128]{2,1,0:T(8,128)} %broadcast_in_dim.16.refs_3_.refs_4_, ...), custom_call_target="tpu_custom_call" | custom-call | flops 83886080 | bytes 2097152 | tf_op jit(solution)/shard_map/scan_forward/pallas_call | solution.py:252
  108.8 8.1 %all-to-all-start = ((bf16[16,64,128]{2,0,1:T(8,128)(2,1)}), bf16[16,64,128]{2,0,1:T(8,128)(2,1)S(1)}, u32[]{:S(2)}, u32[]{:S(2)}) async-start(bf16[16,64,128]{2,0,1:T(8,128)(2,1)} %convert_bitcast_fusion.1), calls=%async_computation | async-start | bytes 524288 | tf_op jit(solution)/shard_map/all_to_all | solution.py:514
  118.5 2.7 fusion.2.refs_9_
  123.0 16.6 %scan_forward.2 = (f32[64,16,128]{2,1,0:T(8,128)}, f32[2,16,16,128]{3,2,1,0:T(8,128)}) custom-call(bf16[64,16,128]{2,1,0:T(8,128)(2,1)} %copy.139.refs_0_, bf16[2,64,16,64]{3,2,1,0:T(8,128)(2,1)} %pad_maximum_fusion.6.refs_1_, bf16[4,64,128]{2,1,0:T(8,128)(2,1)} %pad.4.clone.refs_2_, f32[4,8,128]{2,1,0:T(8,128)} %broadcast_in_dim.16.refs_3_.refs_4_, ...), custom_call_target="tpu_custom_call" | custom-call | flops 83886080 | bytes 2097152 | tf_op jit(solution)/shard_map/scan_forward/pallas_call | solution.py:252
  141.7 3.4 %fusion.56 = (f32[64,16]{0,1:T(8,128)S(1)}, f32[64,16]{0,1:T(8,128)S(1)}, f32[64,16]{0,1:T(8,128)S(1)}, f32[64,16,128]{2,0,1:T(8,128)}) fusion(f32[128]{0:T(128)S(1)} %dynamic_slice.30, bf16[64,16,128]{2,1,0:T(8,128)(2,1)S(1)} %get-tuple-element.82, f32[64,16,128]{2,0,1:T(8,128)S(1)} %get-tuple-element.68, f32[64,16]{0,1:T(8,128)S(1)} %get-tuple-element.110, ...), kind=kOutput, calls=%fused_computation.153 | convolution fusion | flops 135918592 | bytes 2507268 | tf_op jit(solution)/shard_map/dot_general | solution.py:517
  146.0 5.8 %exchange_6.1 = f32[8,32,128]{2,1,0:T(8,128)} custom-call(f32[32,128]{1,0:T(8,128)} %reshape.154.refs_0_), custom_call_target="tpu_custom_call" | custom-call | tf_op jit(solution)/shard_map/exchange_6/pallas_call | solution.py:413
  153.5 2.3 fusion.23
  157.6 1.9 fusion.8
  159.6 14.6 %exchange_7.1 = (bf16[4,16,16,128]{3,2,1,0:T(8,128)(2,1)}, bf16[8,8,16,128]{3,2,1,0:T(8,128)(2,1)}, bf16[4,32,512]{2,1,0:T(8,128)(2,1)}) custom-call(bf16[4,16,16,128]{3,2,1,0:T(8,128)(2,1)} %copy.157.refs_0_, bf16[8,8,16,128]{3,2,1,0:T(8,128)(2,1)} %copy.158.refs_1_, bf16[4,32,512]{2,1,0:T(8,128)(2,1)} %bitcast.208), custom_call_target="tpu_custom_call" | custom-call | tf_op jit(solution)/shard_map/exchange_7/pallas_call | solution.py:413
  175.9 32.7 %scan_backward.2 = (f32[64,16,128]{2,1,0:T(8,128)}, f32[2,64,16,64]{3,2,1,0:T(8,128)}) custom-call(bf16[64,16,128]{2,1,0:T(8,128)(2,1)} %bitcast.212, bf16[2,64,16,64]{3,2,1,0:T(8,128)(2,1)} %pad_maximum_fusion.7.refs_1_, bf16[4,64,128]{2,1,0:T(8,128)(2,1)} %pad.4.clone.refs_2_, bf16[4,128,64]{2,1,0:T(8,128)(2,1)} %pad_bitcast_fusion.refs_3_, ...), custom_call_target="tpu_custom_call" | custom-call | flops 125829120 | bytes 4194304 | tf_op jit(solution)/shard_map/scan_backward/pallas_call | solution.py:287
  212.1 3.7 %all-to-all-start.1 = ((bf16[16,64,256]{2,0,1:T(8,128)(2,1)}), bf16[16,64,256]{2,0,1:T(8,128)(2,1)S(1)}, u32[]{:S(2)}, u32[]{:S(2)}) async-start(bf16[16,64,256]{2,0,1:T(8,128)(2,1)} %maximum_bitcast_fusion), calls=%async_computation.1 | async-start | bytes 1048576 | tf_op jit(solution)/shard_map/all_to_all | solution.py:566
  217.5 12.1 %all-to-all-done.1 = bf16[16,64,256]{2,0,1:T(8,128)(2,1)S(1)} async-done(((bf16[16,64,256]{2,0,1:T(8,128)(2,1)}), bf16[16,64,256]{2,0,1:T(8,128)(2,1)S(1)}, u32[]{:S(2)}, u32[]{:S(2)}) %all-to-all-start.1) | async-done | bytes 524320 | tf_op jit(solution)/shard_map/all_to_all | solution.py:566
  230.7 32.6 %scan_backward.3 = (f32[64,16,128]{2,1,0:T(8,128)}, f32[2,64,16,64]{3,2,1,0:T(8,128)}) custom-call(bf16[64,16,128]{2,1,0:T(8,128)(2,1)} %copy.139.refs_0_, bf16[2,64,16,64]{3,2,1,0:T(8,128)(2,1)} %pad_maximum_fusion.6.refs_1_, bf16[4,64,128]{2,1,0:T(8,128)(2,1)} %pad.4.clone.refs_2_, bf16[4,128,64]{2,1,0:T(8,128)(2,1)} %pad_bitcast_fusion.refs_3_, ...), custom_call_target="tpu_custom_call" | custom-call | flops 125829120 | bytes 4194304 | tf_op jit(solution)/shard_map/scan_backward/pallas_call | solution.py:287
  265.7 12.4 %exchange_9.1 = (bf16[8,8,16,256]{3,2,1,0:T(8,128)(2,1)}, bf16[8,32,512]{2,1,0:T(8,128)(2,1)}) custom-call(bf16[8,8,16,256]{3,2,1,0:T(8,128)(2,1)} %pad_maximum_fusion.8.refs_0_, bf16[32,512]{1,0:T(8,128)(2,1)} %reduce_sum.126.refs_1_), custom_call_target="tpu_custom_call" | custom-call | tf_op jit(solution)/shard_map/exchange_9/pallas_call | solution.py:413
  279.9 9.4 %exchange_10.1 = (bf16[8,8,16,256]{3,2,1,0:T(8,128)(2,1)}, bf16[4,2,32,512]{3,2,1,0:T(8,128)(2,1)}) custom-call(bf16[8,16,256]{2,1,0:T(8,128)(2,1)} %reduce_sum.127.refs_0_, bf16[4,2,32,512]{3,2,1,0:T(8,128)(2,1)} %bitcast.210), custom_call_target="tpu_custom_call" | custom-call | tf_op jit(solution)/shard_map/exchange_10/pallas_call | solution.py:413
  291.6 6.5 %exchange_11.1 = f32[2,64,128]{2,1,0:T(8,128)} custom-call(f32[2,64,128]{2,1,0:T(8,128)} %pad_maximum_fusion.17.refs_0_), custom_call_target="tpu_custom_call" | custom-call | tf_op jit(solution)/shard_map/exchange_11/pallas_call | solution.py:413
  301.5 9.4 %exchange_12.1 = (bf16[8,8,16,256]{3,2,1,0:T(8,128)(2,1)}, bf16[4,128,256]{2,1,0:T(8,128)(2,1)}) custom-call(bf16[8,8,16,256]{3,2,1,0:T(8,128)(2,1)} %bitcast.192, bf16[4,128,256]{2,1,0:T(8,128)(2,1)} %bitcast.209), custom_call_target="tpu_custom_call" | custom-call | tf_op jit(solution)/shard_map/exchange_12/pallas_call | solution.py:413
  316.9 4.3 %exchange_13.1 = bf16[2,128,128]{2,1,0:T(8,128)(2,1)} custom-call(bf16[2,128,128]{2,1,0:T(8,128)(2,1)} %bitcast.218), custom_call_target="tpu_custom_call" | custom-call | tf_op jit(solution)/shard_map/exchange_13/pallas_call | solution.py:413
  322.6 9.2 %exchange_14.1 = bf16[4,128,256]{2,1,0:T(8,128)(2,1)} custom-call(bf16[128,256]{1,0:T(8,128)(2,1)} %pad_maximum_fusion.18.refs_0_), custom_call_target="tpu_custom_call" | custom-call | tf_op jit(solution)/shard_map/exchange_14/pallas_call | solution.py:413
  (172 shorter events, 66.1 us)
Async XLA Ops:
  7.2 50.3 %copy-start = (bf16[1024,256]{1,0:T(8,128)(2,1)S(1)}, bf16[1024,256]{1,0:T(8,128)(2,1)}, u32[]{:S(2)}) copy-start(bf16[1024,256]{1,0:T(8,128)(2,1)} %param.14) | copy-start | bytes 1572868
  7.2 134.5 %all-gather.6.cloned.1.call-start = ((), (), s32[]{:S(2)}) async-start(), calls=%async_computation.3 | async-start | bytes 1310720 | tf_op jit(solution)/shard_map/all_gather | solution.py:493
  40.6 13.2 %copy-start.13 = (f32[128]{0:T(128)}, f32[128]{0:T(128)S(1)}, u32[]{:S(2)}) copy-start(f32[128]{0:T(128)S(1)} %get-tuple-element.98) | copy-start | bytes 1540
  40.6 13.2 %copy-start.15 = (f32[128]{0:T(128)}, f32[128]{0:T(128)S(1)}, u32[]{:S(2)}) copy-start(f32[128]{0:T(128)S(1)} %get-tuple-element.99) | copy-start | bytes 1540
  40.6 13.2 %copy-start.17 = (f32[128]{0:T(128)}, f32[128]{0:T(128)S(1)}, u32[]{:S(2)}) copy-start(f32[128]{0:T(128)S(1)} %get-tuple-element.100) | copy-start | bytes 1540
  40.6 13.2 %copy-start.19 = (f32[128]{0:T(128)}, f32[128]{0:T(128)S(1)}, u32[]{:S(2)}) copy-start(f32[128]{0:T(128)S(1)} %get-tuple-element.101) | copy-start | bytes 1540
  40.6 13.2 %copy-start.21 = (f32[128]{0:T(128)}, f32[128]{0:T(128)S(1)}, u32[]{:S(2)}) copy-start(f32[128]{0:T(128)S(1)} %get-tuple-element.102) | copy-start | bytes 1540
  40.6 13.2 %copy-start.23 = (f32[128]{0:T(128)}, f32[128]{0:T(128)S(1)}, u32[]{:S(2)}) copy-start(f32[128]{0:T(128)S(1)} %get-tuple-element.103) | copy-start | bytes 1540
  40.6 13.2 %copy-start.25 = (f32[128]{0:T(128)}, f32[128]{0:T(128)S(1)}, u32[]{:S(2)}) copy-start(f32[128]{0:T(128)S(1)} %get-tuple-element.104) | copy-start | bytes 1540
  40.6 13.2 %copy-start.27 = (f32[128]{0:T(128)}, f32[128]{0:T(128)S(1)}, u32[]{:S(2)}) copy-start(f32[128]{0:T(128)S(1)} %get-tuple-element.105) | copy-start | bytes 1540
  40.6 13.2 %copy-start.29 = (f32[128]{0:T(128)}, f32[128]{0:T(128)S(1)}, u32[]{:S(2)}) copy-start(f32[128]{0:T(128)S(1)} %get-tuple-element.106) | copy-start | bytes 1540
  55.6 86.1 %all-gather.4.cloned.1.call-start = ((), (), s32[]{:S(2)}) async-start(), calls=%async_computation.2 | async-start | bytes 1179648 | tf_op jit(solution)/shard_map/all_gather | solution.py:492
  106.9 15.0 %copy-start.1 = (bf16[8,8,16,256]{3,2,1,0:T(8,128)(2,1)S(1)}, bf16[8,8,16,256]{3,2,1,0:T(8,128)(2,1)}, u32[]{:S(2)}) copy-start(bf16[8,8,16,256]{3,2,1,0:T(8,128)(2,1)} %exchange_3.1) | copy-start | bytes 1572868
  108.8 31.5 %all-to-all-start = ((bf16[16,64,128]{2,0,1:T(8,128)(2,1)}), bf16[16,64,128]{2,0,1:T(8,128)(2,1)S(1)}, u32[]{:S(2)}, u32[]{:S(2)}) async-start(bf16[16,64,128]{2,0,1:T(8,128)(2,1)} %convert_bitcast_fusion.1), calls=%async_computation | async-start | bytes 524288 | tf_op jit(solution)/shard_map/all_to_all | solution.py:514
  116.9 113.0 %all-gather.8.cloned.1.call-start = ((), (), s32[]{:S(2)}) async-start(), calls=%async_computation.4 | async-start | bytes 2359296 | tf_op jit(solution)/shard_map/all_gather | solution.py:494
  121.9 19.8 %copy-start.31 = (f32[128]{0:T(128)}, f32[128]{0:T(128)S(1)}, u32[]{:S(2)}) copy-start(f32[128]{0:T(128)S(1)} %dynamic_slice.30) | copy-start | bytes 1540
  212.1 17.4 %all-to-all-start.1 = ((bf16[16,64,256]{2,0,1:T(8,128)(2,1)}), bf16[16,64,256]{2,0,1:T(8,128)(2,1)S(1)}, u32[]{:S(2)}, u32[]{:S(2)}) async-start(bf16[16,64,256]{2,0,1:T(8,128)(2,1)} %maximum_bitcast_fusion), calls=%async_computation.1 | async-start | bytes 1048576 | tf_op jit(solution)/shard_map/all_to_all | solution.py:566
  264.7 24.6 %copy-start.9 = (f32[64,16,128]{2,0,1:T(8,128)S(1)}, f32[64,16,128]{2,0,1:T(8,128)}, u32[]{:S(2)}) copy-start(f32[64,16,128]{2,0,1:T(8,128)} %get-tuple-element.70) | copy-start | bytes 1572868
  264.7 24.6 %copy-start.33 = (f32[64,16,128]{2,1,0:T(8,128)S(1)}, f32[64,16,128]{2,1,0:T(8,128)}, u32[]{:S(2)}) copy-start(f32[64,16,128]{2,1,0:T(8,128)} %get-tuple-element.53) | copy-start | bytes 1572868
  290.8 8.1 %copy-start.14 = (f32[128]{0:T(128)S(1)}, f32[128]{0:T(128)}, u32[]{:S(2)}) copy-start(f32[128]{0:T(128)} %copy-done.13) | copy-start | bytes 1540
  290.8 8.1 %copy-start.16 = (f32[128]{0:T(128)S(1)}, f32[128]{0:T(128)}, u32[]{:S(2)}) copy-start(f32[128]{0:T(128)} %copy-done.15) | copy-start | bytes 1540
  301.5 32.1 %copy-start.10 = (bf16[4,2,32,512]{3,2,1,0:T(8,128)(2,1)S(1)}, bf16[4,2,32,512]{3,2,1,0:T(8,128)(2,1)}, u32[]{:S(2)}) copy-start(bf16[4,2,32,512]{3,2,1,0:T(8,128)(2,1)} %get-tuple-element.57) | copy-start | bytes 786436
  312.0 22.5 %copy-start.2 = (bf16[512,2048]{1,0:T(8,128)(2,1)S(1)}, bf16[512,2048]{1,0:T(8,128)(2,1)}, u32[]{:S(2)}) copy-start(bf16[512,2048]{1,0:T(8,128)(2,1)} %all-gather.8.cloned.1.call-done) | copy-start | bytes 6291460
  312.0 22.5 %copy-start.8 = (bf16[8,16,512]{2,1,0:T(8,128)(2,1)S(1)}, bf16[8,16,512]{2,1,0:T(8,128)(2,1)}, u32[]{:S(2)}) copy-start(bf16[8,16,512]{2,1,0:T(8,128)(2,1)} %param.21) | copy-start | bytes 393220
  (15 other events, 90.3 us)
Sparse Core Ops, SparseCore 0:
  55.7 33.9 all-gather.5
  91.6 22.3 all-gather.3
  119.6 29.1 all-gather.7

commit v4 on v3

--- a/solution.py
+++ b/solution.py
@@ -95,7 +95,7 @@
         )
         return state, total + step
 
-    state, total = loop(length, first, ((zero,) * states, zero), 2)
+    state, total = loop(length, first, ((zero,) * states, zero), 4)
     closed = []
     for n in range(states):
         one = state[n] / (1.0 - jnp.exp2(total * rate_ref[n]))
@@ -122,7 +122,7 @@
         y_ref[p] = y
         return tuple(new)
 
-    loop(length, second, tuple(closed), 2)
+    loop(length, second, tuple(closed), 4)
 
 
 def backward_kernel(
@@ -169,7 +169,7 @@
             new.append(one)
         return tuple(new), total + step
 
-    _, total = loop(length, replay, (tuple(start_ref[n] for n in range(states)), zero), 2)
+    _, total = loop(length, replay, (tuple(start_ref[n] for n in range(states)), zero), 4)
 
     def adjoint(j, back):
         i = length - 1 - j
@@ -180,7 +180,7 @@
             decay_at(i, n, step) * (back[n] + gy * coef(p, states + n)) for n in range(states)
         )
 
-    back = loop(length, adjoint, (zero,) * states, 2)
+    back = loop(length, adjoint, (zero,) * states, 4)
     back = tuple(back[n] / (1.0 - jnp.exp2(total * rate_ref[n])) for n in range(states))
 
     @pl.when(k == 0)
@@ -477,18 +477,20 @@
             convolved = convolved + padded[a : a + all_rows, b : b + cols].astype(F32) * taps[a, b]
     active = jax.nn.silu(convolved).astype(BF16)
 
-    act_row, act_col = exchange(
-        2, ("spread", "row", parts(active, 0, nr)), ("spread", "col", parts(active, 0, nc))
-    )
+    (act_row,) = exchange(2, ("spread", "row", parts(active, 0, nr)))
     act_cells = joined(act_row, 2)
     proj_cells = jnp.dot(act_cells.reshape(-1, e_dim), proj_weight, preferred_element_type=F32)
     split = 2 * coefs
-    (proj,) = exchange(3, ("gather", "row", proj_cells.astype(BF16).reshape(rows, cols, 2 * split)))
+    proj, act_col = exchange(
+        3,
+        ("gather", "row", proj_cells.astype(BF16).reshape(rows, cols, 2 * split)),
+        ("spread", "col", parts(active, 0, nc)),
+    )
     proj = proj.reshape(all_rows, cols, 2 * split)
     (proj_col,) = exchange(4, ("spread", "col", parts(proj[..., split:], 0, nc)))
     act_down = active
     act_across, across = swap(joined(act_col, 1)), swap(joined(proj_col, 1))
-    act_across, later_grad, later_out, later_w = lax.optimization_barrier((act_across, grad_out, out_weight, w_mine))
+    across, later_grad, later_out, later_w = lax.optimization_barrier((across, grad_out, out_weight, w_mine))
     grad_all = lax.all_gather(later_grad, "row", axis=0, tiled=True)
     out_full = lax.all_gather(later_out, "col", axis=0, tiled=True)
     w_perm = lax.all_gather(later_w, "row", axis=1, tiled=True)
@@ -548,15 +550,11 @@
     out_part = lax.dot_general(
         mixed.reshape(-1, width), grad_all.reshape(-1, c_dim), contract, preferred_element_type=F32
     )
-    gy_across, mixed_cells, out_parts = exchange(
-        7,
-        ("spread", "col", parts(back_bf, 0, nc)),
-        ("spread", "row", parts(mixed, 0, nr)),
-        ("spread", "col", parts(out_part.astype(BF16), 0, nc)),
+    gy_across, mixed_cells = exchange(
+        7, ("spread", "col", parts(back_bf, 0, nc)), ("spread", "row", parts(mixed, 0, nr))
     )
     gy_across = swap(joined(gy_across, 1))
     mixed_cells = joined(mixed_cells, 2).reshape(-1, e_dim)
-    out_sum = jnp.sum(out_parts.astype(F32), axis=0).astype(BF16)
 
     dact_across, dproj_across = run_backward(
         act_across, proj_across, params_across, start_across, pad_to(gy_across, 2, lanes), pick, spread
@@ -564,17 +562,18 @@
     unpair = lambda values: jnp.concatenate([values[0], values[1]], axis=-1)
     returned = swap(jnp.concatenate([dact_across[..., :width], unpair(dproj_across)], axis=-1).astype(BF16))
     returned = lax.all_to_all(returned, "col", 1, 0, tiled=True)
-    back_bf, w_perm, dact_across = lax.optimization_barrier((back_bf, w_perm, dact_across))
     dact_down, dproj_down = run_backward(
         act_down, proj_down, params_down, start_down, pad_to(back_bf, 2, lanes), pick, spread
     )
     dproj = jnp.concatenate([unpair(dproj_down), returned[..., width:].astype(F32)], axis=-1)
-    dproj, out_rows = exchange(
-        9, ("spread", "row", parts(dproj.astype(BF16), 0, nr)), ("gather", "row", out_sum)
-    )
+    dproj, out_parts = exchange(
+        9,
+        ("spread", "row", parts(dproj.astype(BF16), 0, nr)),
+        ("spread", "col", parts(out_part.astype(BF16), 0, nc)),
+    )
+    out_sum = jnp.sum(out_parts.astype(F32), axis=0).astype(BF16)
     dproj = jnp.sum(dproj.astype(F32), axis=0).astype(BF16)
-    dproj, out_own = exchange(10, ("gather", "row", dproj), ("spread", "col", parts(out_rows, 0, nc)))
-    grad_out_w = jnp.swapaxes(out_own, 0, 1).reshape(e_dim // nc, c_dim)
+    dproj, out_rows = exchange(10, ("gather", "row", dproj), ("gather", "row", out_sum))
     proj_rows = lax.dynamic_slice_in_dim(proj_weight, me * width, width, axis=0)
     back_active = lax.dot_general(
         dproj.reshape(-1, dirs * coefs), proj_rows, (((1,), (1,)), ((), ())), preferred_element_type=F32
@@ -582,7 +581,10 @@
     back_active = back_active + dact_down[..., :width] + returned[..., :width].astype(F32)
     conv_sig = jax.nn.sigmoid(convolved)
     back_conv = back_active * (conv_sig * (1.0 + convolved * (1.0 - conv_sig)))
-    (conv_edges,) = exchange(11, ("halo", "col", edges(back_conv)))
+    conv_edges, out_own = exchange(
+        11, ("halo", "col", edges(back_conv)), ("spread", "col", parts(out_rows, 0, nc))
+    )
+    grad_out_w = jnp.swapaxes(out_own, 0, 1).reshape(e_dim // nc, c_dim)
     grad_padded = with_edges(back_conv, conv_edges)
     back_source = jnp.zeros(source.shape, F32)
     for a in range(3):

time: 344 us -> 318 us (0.924)
  waiting for transfers between devices: 13.5 us -> 1.47 us
  Pallas kernels: 228 us -> 222 us
  starting transfers between devices: 11.8 us -> 7.93 us
    all_to_all x1, waiting for transfers between devices: 12.1 us -> 0.01 us  [local(): returned = lax.all_to_all(returned, 'col', 1, 0, tiled=True)]
    all_to_all x1, starting transfers between devices: 8.06 us -> 3.99 us  [local(): lax.all_to_all(swap(y_across[..., :width].astype(BF16)), 'col', 1, 0, til...]
  transfers between devices with their start and end apart: 5 -> 5, of which waited for: 1 -> 0; matrix products, arithmetic and copies ran while one was open for 12% -> 16% of each run, Pallas kernels for 32% -> 54%
where the time goes in v4:
time: 318 us; the launch traced here: 316 us
  Pallas kernels  222 us (70%)
  local copies, waits for them, and re-layouts  29.7 us (9%)
  other arithmetic  26.6 us (8%)
  between operations  14.3 us (4%)
  matrix products  14.1 us (4%)
  starting transfers between devices  7.93 us (2%)
    pallas_call x13, Pallas kernels, exchange(): pl.pallas_call(lambda *refs: exchange_kernel(plan, sizes, *refs), in_spec...  127 us
    pallas_call x2, Pallas kernels, run_backward(): pl.pallas_call(lambda *refs: backward_kernel(states, *refs), grid=(2,), i...  63.9 us
    pallas_call x2, Pallas kernels, run_forward(): pl.pallas_call(lambda *refs: forward_kernel(states, *refs), grid=(2,), in...  31.8 us
  transfers between devices with their start and end apart: 5, of which 0 were waited for; matrix products, arithmetic and copies ran while one was open for 16% of the time, Pallas kernels for 54%

profile of v4, /device:TPU:0, one launch (start us, length us, event | category | flops | bytes accessed | tf_op | source)
XLA Modules:
  0.0 316.3 jit_solution(15564228962964983310)
XLA Ops:
  9.2 18.7 %exchange_0.1 = (bf16[2,512,128]{2,1,0:T(8,128)(2,1)}, bf16[8,8,16,512]{3,2,1,0:T(8,128)(2,1)}) custom-call(bf16[2,512,128]{2,1,0:T(8,128)(2,1)} %bitcast.199, bf16[8,16,512]{2,1,0:T(8,128)(2,1)} %refs_1_.1), custom_call_target="tpu_custom_call" | custom-call | tf_op jit(solution)/shard_map/exchange_0/pallas_call | solution.py:413
  32.1 6.6 %exchange_1.1 = bf16[2,64,128]{2,1,0:T(8,128)(2,1)} custom-call(bf16[2,64,128]{2,1,0:T(8,128)(2,1)} %pad_maximum_fusion.19.refs_0_), custom_call_target="tpu_custom_call" | custom-call | tf_op jit(solution)/shard_map/exchange_1/pallas_call | solution.py:413
  42.7 6.9 %exchange_2.1 = bf16[8,8,16,128]{3,2,1,0:T(8,128)(2,1)} custom-call(bf16[8,8,16,128]{3,2,1,0:T(8,128)(2,1)} %copy.135.refs_0_), custom_call_target="tpu_custom_call" | custom-call | tf_op jit(solution)/shard_map/exchange_2/pallas_call | solution.py:413
  52.5 11.0 %exchange_3.1 = (bf16[8,8,16,256]{3,2,1,0:T(8,128)(2,1)}, bf16[4,16,16,128]{3,2,1,0:T(8,128)(2,1)}) custom-call(bf16[8,16,256]{2,1,0:T(8,128)(2,1)} %bitcast.219, bf16[4,16,16,128]{3,2,1,0:T(8,128)(2,1)} %copy.137.refs_1_), custom_call_target="tpu_custom_call" | custom-call | tf_op jit(solution)/shard_map/exchange_3/pallas_call | solution.py:413
  65.3 9.0 %exchange_4.1 = bf16[4,16,16,128]{3,2,1,0:T(8,128)(2,1)} custom-call(bf16[4,16,16,128]{3,2,1,0:T(8,128)(2,1)} %bitcast.204), custom_call_target="tpu_custom_call" | custom-call | tf_op jit(solution)/shard_map/exchange_4/pallas_call | solution.py:413
  83.9 15.9 %scan_forward.3 = (f32[64,16,128]{2,1,0:T(8,128)}, f32[2,16,16,128]{3,2,1,0:T(8,128)}) custom-call(bf16[64,16,128]{2,1,0:T(8,128)(2,1)} %bitcast.212, bf16[2,64,16,64]{3,2,1,0:T(8,128)(2,1)} %pad_maximum_fusion.7.refs_1_, bf16[4,64,128]{2,1,0:T(8,128)(2,1)} %pad.4.clone.refs_2_, f32[4,8,128]{2,1,0:T(8,128)} %broadcast_in_dim.16.refs_3_.refs_4_, ...), custom_call_target="tpu_custom_call" | custom-call | flops 83886080 | bytes 2097152 | tf_op jit(solution)/shard_map/scan_forward/pallas_call | solution.py:252
  99.8 1.8 convert_bitcast_fusion.1
  101.6 4.0 %all-to-all-start = ((bf16[16,64,128]{2,0,1:T(8,128)(2,1)}), bf16[16,64,128]{2,0,1:T(8,128)(2,1)S(1)}, u32[]{:S(2)}, u32[]{:S(2)}) async-start(bf16[16,64,128]{2,0,1:T(8,128)(2,1)} %convert_bitcast_fusion.1), calls=%async_computation | async-start | bytes 524288 | tf_op jit(solution)/shard_map/all_to_all | solution.py:516
  107.2 2.7 fusion.2.refs_9_
  111.8 15.9 %scan_forward.2 = (f32[64,16,128]{2,1,0:T(8,128)}, f32[2,16,16,128]{3,2,1,0:T(8,128)}) custom-call(bf16[64,16,128]{2,1,0:T(8,128)(2,1)} %copy.139.refs_0_, bf16[2,64,16,64]{3,2,1,0:T(8,128)(2,1)} %pad_maximum_fusion.6.refs_1_, bf16[4,64,128]{2,1,0:T(8,128)(2,1)} %pad.4.clone.refs_2_, f32[4,8,128]{2,1,0:T(8,128)} %broadcast_in_dim.16.refs_3_.refs_4_, ...), custom_call_target="tpu_custom_call" | custom-call | flops 83886080 | bytes 2097152 | tf_op jit(solution)/shard_map/scan_forward/pallas_call | solution.py:252
  129.8 2.8 fusion.56
  133.5 5.6 %exchange_6.1 = f32[8,32,128]{2,1,0:T(8,128)} custom-call(f32[32,128]{1,0:T(8,128)} %reshape.154.refs_0_), custom_call_target="tpu_custom_call" | custom-call | tf_op jit(solution)/shard_map/exchange_6/pallas_call | solution.py:413
  143.4 11.1 %exchange_7.1 = (bf16[4,16,16,128]{3,2,1,0:T(8,128)(2,1)}, bf16[8,8,16,128]{3,2,1,0:T(8,128)(2,1)}) custom-call(bf16[4,16,16,128]{3,2,1,0:T(8,128)(2,1)} %copy.156.refs_0_, bf16[8,8,16,128]{3,2,1,0:T(8,128)(2,1)} %copy.157.refs_1_), custom_call_target="tpu_custom_call" | custom-call | tf_op jit(solution)/shard_map/exchange_7/pallas_call | solution.py:413
  156.2 32.0 %scan_backward.3 = (f32[64,16,128]{2,1,0:T(8,128)}, f32[2,64,16,64]{3,2,1,0:T(8,128)}) custom-call(bf16[64,16,128]{2,1,0:T(8,128)(2,1)} %bitcast.213, bf16[2,64,16,64]{3,2,1,0:T(8,128)(2,1)} %pad_maximum_fusion.7.refs_1_, bf16[4,64,128]{2,1,0:T(8,128)(2,1)} %pad.4.clone.refs_2_, bf16[4,128,64]{2,1,0:T(8,128)(2,1)} %pad_bitcast_fusion.refs_3_, ...), custom_call_target="tpu_custom_call" | custom-call | flops 125829120 | bytes 4194304 | tf_op jit(solution)/shard_map/scan_backward/pallas_call | solution.py:287
  190.6 3.9 %all-to-all-start.1 = ((bf16[16,64,256]{2,0,1:T(8,128)(2,1)}), bf16[16,64,256]{2,0,1:T(8,128)(2,1)S(1)}, u32[]{:S(2)}, u32[]{:S(2)}) async-start(bf16[16,64,256]{2,0,1:T(8,128)(2,1)} %maximum_bitcast_fusion), calls=%async_computation.1 | async-start | bytes 1048576 | tf_op jit(solution)/shard_map/all_to_all | solution.py:564
  195.4 31.9 %scan_backward.2 = (f32[64,16,128]{2,1,0:T(8,128)}, f32[2,64,16,64]{3,2,1,0:T(8,128)}) custom-call(bf16[64,16,128]{2,1,0:T(8,128)(2,1)} %copy.139.refs_0_, bf16[2,64,16,64]{3,2,1,0:T(8,128)(2,1)} %pad_maximum_fusion.6.refs_1_, bf16[4,64,128]{2,1,0:T(8,128)(2,1)} %pad.4.clone.refs_2_, bf16[4,128,64]{2,1,0:T(8,128)(2,1)} %pad_bitcast_fusion.refs_3_, ...), custom_call_target="tpu_custom_call" | custom-call | flops 125829120 | bytes 4194304 | tf_op jit(solution)/shard_map/scan_backward/pallas_call | solution.py:287
  228.8 1.9 fusion.8
  233.1 10.7 %exchange_9.1 = (bf16[8,8,16,256]{3,2,1,0:T(8,128)(2,1)}, bf16[4,32,512]{2,1,0:T(8,128)(2,1)}) custom-call(bf16[8,8,16,256]{3,2,1,0:T(8,128)(2,1)} %pad_maximum_fusion.8.refs_0_, bf16[4,32,512]{2,1,0:T(8,128)(2,1)} %bitcast.209), custom_call_target="tpu_custom_call" | custom-call | tf_op jit(solution)/shard_map/exchange_9/pallas_call | solution.py:413
  247.1 13.1 %exchange_10.1 = (bf16[8,8,16,256]{3,2,1,0:T(8,128)(2,1)}, bf16[8,32,512]{2,1,0:T(8,128)(2,1)}) custom-call(bf16[8,16,256]{2,1,0:T(8,128)(2,1)} %reduce_sum.126.refs_0_, bf16[32,512]{1,0:T(8,128)(2,1)} %reduce_sum.127.refs_1_), custom_call_target="tpu_custom_call" | custom-call | tf_op jit(solution)/shard_map/exchange_10/pallas_call | solution.py:413
  262.5 10.5 %exchange_11.1 = (f32[2,64,128]{2,1,0:T(8,128)}, bf16[4,2,32,512]{3,2,1,0:T(8,128)(2,1)}) custom-call(f32[2,64,128]{2,1,0:T(8,128)} %pad_maximum_fusion.17.refs_0_, bf16[4,2,32,512]{3,2,1,0:T(8,128)(2,1)} %bitcast.211), custom_call_target="tpu_custom_call" | custom-call | tf_op jit(solution)/shard_map/exchange_11/pallas_call | solution.py:413
  276.2 9.7 %exchange_12.1 = (bf16[8,8,16,256]{3,2,1,0:T(8,128)(2,1)}, bf16[4,128,256]{2,1,0:T(8,128)(2,1)}) custom-call(bf16[8,8,16,256]{3,2,1,0:T(8,128)(2,1)} %bitcast.190, bf16[4,128,256]{2,1,0:T(8,128)(2,1)} %bitcast.210), custom_call_target="tpu_custom_call" | custom-call | tf_op jit(solution)/shard_map/exchange_12/pallas_call | solution.py:413
  288.9 4.5 %exchange_13.1 = bf16[2,128,128]{2,1,0:T(8,128)(2,1)} custom-call(bf16[2,128,128]{2,1,0:T(8,128)(2,1)} %bitcast.218), custom_call_target="tpu_custom_call" | custom-call | tf_op jit(solution)/shard_map/exchange_13/pallas_call | solution.py:413
  294.9 9.1 %exchange_14.1 = bf16[4,128,256]{2,1,0:T(8,128)(2,1)} custom-call(bf16[128,256]{1,0:T(8,128)(2,1)} %pad_maximum_fusion.18.refs_0_), custom_call_target="tpu_custom_call" | custom-call | tf_op jit(solution)/shard_map/exchange_14/pallas_call | solution.py:413
  306.6 3.1 fusion.5
  (132 shorter events, 59.5 us)
Async XLA Ops:
  7.2 44.5 %copy-start = (bf16[1024,256]{1,0:T(8,128)(2,1)S(1)}, bf16[1024,256]{1,0:T(8,128)(2,1)}, u32[]{:S(2)}) copy-start(bf16[1024,256]{1,0:T(8,128)(2,1)} %param.14) | copy-start | bytes 1572868
  7.2 122.6 %all-gather.6.cloned.1.call-start = ((), (), s32[]{:S(2)}) async-start(), calls=%async_computation.3 | async-start | bytes 1310720 | tf_op jit(solution)/shard_map/all_gather | solution.py:495
  63.6 12.6 %copy-start.10 = (bf16[4,16,16,128]{3,2,1,0:T(8,128)(2,1)S(1)}, bf16[4,16,16,128]{3,2,1,0:T(8,128)(2,1)}, u32[]{:S(2)}) copy-start(bf16[4,16,16,128]{3,2,1,0:T(8,128)(2,1)} %get-tuple-element.34) | copy-start | bytes 786436
  75.4 54.4 %all-gather.4.cloned.1.call-start = ((), (), s32[]{:S(2)}) async-start(), calls=%async_computation.2 | async-start | bytes 1179648 | tf_op jit(solution)/shard_map/all_gather | solution.py:494
  99.8 10.9 %copy-start.2 = (bf16[8,8,16,256]{3,2,1,0:T(8,128)(2,1)S(1)}, bf16[8,8,16,256]{3,2,1,0:T(8,128)(2,1)}, u32[]{:S(2)}) copy-start(bf16[8,8,16,256]{3,2,1,0:T(8,128)(2,1)} %get-tuple-element.32) | copy-start | bytes 1572868
  101.6 26.8 %all-to-all-start = ((bf16[16,64,128]{2,0,1:T(8,128)(2,1)}), bf16[16,64,128]{2,0,1:T(8,128)(2,1)S(1)}, u32[]{:S(2)}, u32[]{:S(2)}) async-start(bf16[16,64,128]{2,0,1:T(8,128)(2,1)} %convert_bitcast_fusion.1), calls=%async_computation | async-start | bytes 524288 | tf_op jit(solution)/shard_map/all_to_all | solution.py:516
  105.6 201.0 %all-gather.8.cloned.1.call-start = ((), (), s32[]{:S(2)}) async-start(), calls=%async_computation.4 | async-start | bytes 2359296 | tf_op jit(solution)/shard_map/all_gather | solution.py:496
  188.2 1.4 copy-start.7
  190.6 41.1 %all-to-all-start.1 = ((bf16[16,64,256]{2,0,1:T(8,128)(2,1)}), bf16[16,64,256]{2,0,1:T(8,128)(2,1)S(1)}, u32[]{:S(2)}, u32[]{:S(2)}) async-start(bf16[16,64,256]{2,0,1:T(8,128)(2,1)} %maximum_bitcast_fusion), calls=%async_computation.1 | async-start | bytes 1048576 | tf_op jit(solution)/shard_map/all_to_all | solution.py:564
  227.3 1.5 copy-start.4
  227.3 3.5 %copy-start.3 = (bf16[1024,512]{1,0:T(8,128)(2,1)S(1)}, bf16[1024,512]{1,0:T(8,128)(2,1)}, u32[]{:S(2)}) copy-start(bf16[1024,512]{1,0:T(8,128)(2,1)} %all-gather.6.cloned.1.call-done) | copy-start | bytes 3145732
  227.3 3.5 %copy-start.5 = (bf16[8,16,512]{2,1,0:T(8,128)(2,1)S(1)}, bf16[8,16,512]{2,1,0:T(8,128)(2,1)}, u32[]{:S(2)}) copy-start(bf16[8,16,512]{2,1,0:T(8,128)(2,1)} %refs_1_.1) | copy-start | bytes 393220
  227.3 3.5 %copy-start.11 = (bf16[8,8,16,128]{3,2,1,0:T(8,128)(2,1)S(1)}, bf16[8,8,16,128]{3,2,1,0:T(8,128)(2,1)}, u32[]{:S(2)}) copy-start(bf16[8,8,16,128]{3,2,1,0:T(8,128)(2,1)} %get-tuple-element.39) | copy-start | bytes 786436
  231.8 28.5 %copy-start.8 = (f32[64,16,128]{2,0,1:T(8,128)S(1)}, f32[64,16,128]{2,0,1:T(8,128)}, u32[]{:S(2)}) copy-start(f32[64,16,128]{2,0,1:T(8,128)} %get-tuple-element.68) | copy-start | bytes 1572868
  231.8 28.5 %copy-start.13 = (f32[64,16,128]{2,1,0:T(8,128)S(1)}, f32[64,16,128]{2,1,0:T(8,128)}, u32[]{:S(2)}) copy-start(f32[64,16,128]{2,1,0:T(8,128)} %get-tuple-element.49) | copy-start | bytes 1572868
  273.8 1.2 copy-start.12
  274.6 1.7 copy-start.1
  276.2 27.7 %copy-start.9 = (bf16[4,2,32,512]{3,2,1,0:T(8,128)(2,1)S(1)}, bf16[4,2,32,512]{3,2,1,0:T(8,128)(2,1)}, u32[]{:S(2)}) copy-start(bf16[4,2,32,512]{3,2,1,0:T(8,128)(2,1)} %get-tuple-element.55) | copy-start | bytes 786436
  287.0 19.6 %copy-start.6 = (bf16[8,16,512]{2,1,0:T(8,128)(2,1)S(1)}, bf16[8,16,512]{2,1,0:T(8,128)(2,1)}, u32[]{:S(2)}) copy-start(bf16[8,16,512]{2,1,0:T(8,128)(2,1)} %param.21) | copy-start | bytes 393220
Sparse Core Ops, SparseCore 0:
  75.5 27.3 all-gather.5
  104.8 23.0 all-gather.3
  129.7 29.8 all-gather.7
